TPU v7x, 768 devices: a whole 4x8x12 slice. The times are simulated.
768 devices in a mesh: grp: 64 (over y, z_hi, core), dom: 12 (over x, z_lo).
Axes of the slice: x: 4, y: 8, z: 12 (z_hi: 4, z_lo: 3; z = z_hi * 3 + z_lo), core: 2. Of those that a mesh axis runs over, the one named last changes fastest.
Arguments:
- grids: float32 [128, 8, 64, 1536], P('grp', None, None, 'dom'), may hold values from -6 to 6
- table: int32 [128, 8], P('grp'), may hold values from 0 to 63, all different within a row
- coefs: int32 [128], P('grp'), may hold values from -10 to 10, as said below
Outputs:
- combined: float32 [128, 8, 64, 1536], P('grp', None, None, 'dom')
Inputs may be any that keep to these rules, and one draw needn't show every extreme that they name: The 8 entries of a row of table differ, and every subspace is named by some row. `coefs`: every coefficient is one of 1, -5, 10, -10, 5, -1.
All inputs are finite; a program needn't handle non-finite values.
Results may differ from a plain program's by a relative error of at most 0.00007.
Values sent between devices are 32-bit elements; how exact they have to be, the bound alone decides.
No kernel may reach another device: no remote copies, remote signals or barrier semaphores. Data moves between devices by JAX's collectives and lax.ppermute only.
A program may use at most 32 MiB of HBM per device.

v0:
```python
import jax
import jax.numpy as jnp
from jax import lax
from jax.sharding import PartitionSpec as P

SUB_DEV = 1


def in_blocks(value, dim, size):
    before, after = (value.shape[:dim], value.shape[dim + 1 :])
    return jnp.moveaxis(value.reshape(*before, size, -1, *after), dim, 0)


def summed_on_arrival(value, axis, dim):
    size = lax.axis_size(axis)
    parts = lax.all_to_all(in_blocks(value, dim, size), axis, 0, 0, tiled=True)
    return jnp.sum(parts, axis=0)


def from_everyone(value, axis):
    size = lax.axis_size(axis)
    return lax.all_to_all(
        jnp.broadcast_to(value[None], (size, *value.shape)), axis, 0, 0, tiled=True
    )


def joined_along(parts, dim):
    parts = jnp.moveaxis(parts, 0, dim)
    dims = parts.shape
    return parts.reshape(*dims[:dim], dims[dim] * dims[dim + 1], *dims[dim + 2 :])


def gather_directly(value, axis, dim):
    parts = from_everyone(value, axis)
    return joined_along(parts, dim)


def on_device(grids, table, coefs):
    local_grids, slots, fields, points = grids.shape
    count = local_grids * slots
    data = grids.reshape(count, fields * points)
    weight = jnp.repeat(coefs.astype(jnp.float32), slots)
    labels = table.reshape(count)
    wanted = jnp.arange(SUB_DEV * lax.axis_size("grp"), dtype=jnp.int32)
    onehot = (labels[None, :] == wanted[:, None]).astype(jnp.float32) * weight[None, :]
    share = summed_on_arrival(
        jnp.dot(onehot, data, precision=lax.Precision.HIGHEST, preferred_element_type=jnp.float32),
        "grp",
        0,
    )
    piece = gather_directly(share, "grp", 0)
    wanted = jnp.arange(piece.shape[0], dtype=jnp.int32)
    picker = (labels[:, None] == wanted[None, :]).astype(jnp.float32)
    result = jnp.dot(
        picker, piece, precision=lax.Precision.HIGHEST, preferred_element_type=jnp.float32
    )
    return result.reshape(local_grids, slots, fields, points)


def solution(mesh):
    return jax.shard_map(
        on_device,
        mesh=mesh,
        in_specs=(P("grp", None, None, "dom"), P("grp", None), P("grp")),
        out_specs=P("grp", None, None, "dom"),
        check_vma=False,
    )
```

profile of v0, /device:TPU:144, one launch (start us, length us, event | category | flops | bytes accessed | tf_op | source)
XLA Modules:
  0.0 204.3 jit_solution(5956113071358502088)
XLA Ops:
  0.0 0.7 convert_element_type.2
  0.7 0.1 broadcast_in_dim.4
  0.7 0.1 mul.10
  0.8 0.8 eq.48
  1.6 2.9 %convolution_bitcast_fusion = f32[64,1,8192]{2,0,1:T(8,128)S(1)} fusion(f32[2,8,64,128]{3,2,1,0:T(8,128)} %param.3, f32[16]{0:T(128)S(1)} %mul.10, s32[16]{0:T(128)S(1)} %eq.48), kind=kOutput, calls=%fused_computation | convolution fusion | flops 100665344 | bytes 2621568 | tf_op jit(solution)/shard_map/dot_general | solution.py:47
  4.4 2.2 %copy.7 = f32[64,1,8192]{2,1,0:T(1,128)S(1)} copy(f32[64,1,8192]{2,0,1:T(8,128)S(1)} %convolution_bitcast_fusion) | data formatting | bytes 4194304 | tf_op jit(solution)/shard_map/reshape | solution.py:11
  6.6 94.6 %all_to_all.10 = f32[64,1,8192]{2,1,0:T(1,128)S(1)} all-to-all(f32[64,1,8192]{2,1,0:T(1,128)S(1)} %copy.7), channel_id=1, replica_groups=mesh['grp'=64,'dom'=12] {'grp'}, dimensions={0} | all-to-all | bytes 4194304 | tf_op jit(solution)/shard_map/all_to_all | solution.py:16
  101.2 1.8 reduce_sum.9
  103.0 2.0 broadcast_in_dim.5
  105.0 0.0 copy-start
  105.0 96.5 %all_to_all.11 = f32[64,1,8192]{2,1,0:T(1,128)S(1)} all-to-all(f32[64,1,8192]{2,1,0:T(1,128)S(1)} %broadcast_in_dim.5), channel_id=1, replica_groups=mesh['grp'=64,'dom'=12] {'grp'}, dimensions={0} | all-to-all | bytes 4194304 | tf_op jit(solution)/shard_map/all_to_all | solution.py:22
  201.5 0.0 copy-done
  201.5 2.0 fusion
  203.4 0.9 copy.9
Async XLA Ops:
  105.0 96.5 %copy-start = (s32[2,8]{1,0:T(2,128)S(1)}, s32[2,8]{1,0:T(2,128)}, u32[]{:S(2)}) copy-start(s32[2,8]{1,0:T(2,128)} %param.4) | copy-start | bytes 196
where the time goes:
time: 205 us; the launch traced here: 204 us
  blocking collectives  191 us (93%)
  local copies, waits for them, and re-layouts  5.99 us (3%)
  matrix products  4.82 us (2%)
  other arithmetic  2.44 us (1%)
    all_to_all x1, blocking collectives, from_everyone(): lax.all_to_all(jnp.broadcast_to(value[None], (size, *value.shape)), axis,...  96.5 us
    all_to_all x1, blocking collectives, summed_on_arrival(): parts = lax.all_to_all(in_blocks(value, dim, size), axis, 0, 0, tiled=True)  94.6 us

commit v1 on v0

v1 whole, which is shorter than its diff:
```python
import jax
import jax.numpy as jnp
from jax import lax
from jax.sharding import PartitionSpec as P

SUBS = 64


def on_device(grids, table, coefs):
    local_grids, slots, fields, points = grids.shape
    count = local_grids * slots
    size = lax.axis_size("grp")
    rows = fields // size
    known = jnp.concatenate([table.reshape(count), jnp.repeat(coefs, slots)])
    known = lax.all_gather(known, "grp").reshape(size, 2, count)
    labels = known[:, 0].reshape(size * count)
    weight = known[:, 1].reshape(size * count).astype(jnp.float32)
    sent = grids.reshape(count, size, rows, points).transpose(1, 0, 2, 3)
    parts = lax.all_to_all(sent, "grp", 0, 0, tiled=True)
    parts = parts.reshape(size * count, rows * points)
    wanted = jnp.arange(SUBS, dtype=jnp.int32)
    onehot = (labels[None, :] == wanted[:, None]).astype(jnp.float32)
    sparse = jnp.dot(
        onehot * weight[None, :],
        parts,
        precision=lax.Precision.HIGHEST,
        preferred_element_type=jnp.float32,
    )
    picks = jnp.dot(
        onehot.T, sparse, precision=lax.Precision.HIGHEST, preferred_element_type=jnp.float32
    )
    back = lax.all_to_all(picks.reshape(size, count, rows, points), "grp", 0, 0, tiled=True)
    return back.transpose(1, 0, 2, 3).reshape(local_grids, slots, fields, points)


def solution(mesh):
    return jax.shard_map(
        on_device,
        mesh=mesh,
        in_specs=(P("grp", None, None, "dom"), P("grp", None), P("grp")),
        out_specs=P("grp", None, None, "dom"),
        check_vma=False,
    )
```

time: 205 us -> 101 us (0.49)
  the two profiles are of different devices: /device:TPU:144 before, /device:TPU:69 now
where the time goes in v1:
time: 101 us
  blocking collectives  72.3 us (72%)
  starting transfers between devices  20.1 us (20%)
  local copies, waits for them, and re-layouts  6.28 us (6%)
  matrix products  1.06 us (1%)
    all_to_all x1, blocking collectives, on_device(): lax.all_to_all(picks.reshape(size, count, rows, points), 'grp', 0, 0, til...  40.7 us
    unnamed x1, blocking collectives  31.7 us
    all_to_all x1, starting transfers between devices, on_device(): parts = lax.all_to_all(sent, 'grp', 0, 0, tiled=True)  20.1 us
    unnamed x7, local copies, waits for them, and re-layouts  4.73 us
  transfers between devices with their start and end apart: 1, of which 0 were waited for; matrix products, arithmetic and copies ran while one was open for 2% of the time, Pallas kernels for 0%

profile of v1, /device:TPU:69, one launch (start us, length us, event | category | flops | bytes accessed | tf_op | source)
XLA Modules:
  0.0 100.9 jit_solution(9637549897448741737)
XLA Ops:
  0.0 2.1 %copy.11 = f32[2,8,64,128]{3,1,0,2:T(8,128)} copy(f32[2,8,64,128]{3,2,1,0:T(8,128)} %param.3) | data formatting | bytes 1048576 | tf_op args[0]
  2.1 20.1 %all-to-all-start = ((f32[64,16,1,128]{3,1,2,0:T(8,128)}), f32[64,16,1,128]{3,1,2,0:T(8,128)S(1)}, u32[]{:S(2)}, u32[]{:S(2)}) async-start(f32[64,16,1,128]{3,1,2,0:T(8,128)} %bitcast.14), calls=%async_computation | async-start | bytes 1048576 | tf_op jit(solution)/shard_map/all_to_all | solution.py:19
  22.3 0.0 copy-start.1
  22.3 0.6 copy-done.1
  22.9 0.1 broadcast_in_dim.2
  23.0 0.0 copy-start
  23.0 0.1 reshape.29
  23.1 0.6 copy-done
  23.7 0.1 reshape.28
  23.7 1.3 %dynamic-slice = u32[1]{0:T(128)} dynamic-slice(u32[768]{0:T(1024)} %constant.7, u32[]{:T(128)S(6)} %add), dynamic_slice_sizes={1} | dynamic-slice | bytes 12
  25.8 0.2 add_dynamic-update-slice_fusion
  26.0 31.7 %all-reduce = s32[2048]{0:T(1024)S(1)} all-reduce(s32[2048]{0:T(1024)S(1)} %add_dynamic-update-slice_fusion), channel_id=2, replica_groups=mesh['grp'=64,'dom'=12] {'grp'}, use_global_device_ids=true, to_apply=%add | all-reduce | flops 2048 | bytes 16384
  57.7 0.1 reshape.30
  57.8 0.1 fusion.7
  57.9 0.1 convert_element_type.12
  58.0 0.1 slice_reduce_fusion
  58.1 0.1 eq.15
  58.2 0.0 all-to-all-done
  58.2 0.5 fusion
  58.6 0.6 fusion.2
  59.2 40.7 %all_to_all.10 = f32[64,16,1,128]{3,1,2,0:T(8,128)S(1)} all-to-all(f32[64,16,1,128]{3,1,2,0:T(8,128)S(1)} %bitcast.16), channel_id=1, replica_groups=mesh['grp'=64,'dom'=12] {'grp'}, dimensions={0} | all-to-all | bytes 1048576 | tf_op jit(solution)/shard_map/all_to_all | solution.py:32
  99.9 1.0 copy.9
  (1 shorter events, 0.0 us)
Async XLA Ops:
  2.1 56.0 %all-to-all-start = ((f32[64,16,1,128]{3,1,2,0:T(8,128)}), f32[64,16,1,128]{3,1,2,0:T(8,128)S(1)}, u32[]{:S(2)}, u32[]{:S(2)}) async-start(f32[64,16,1,128]{3,1,2,0:T(8,128)} %bitcast.14), calls=%async_computation | async-start | bytes 1048576 | tf_op jit(solution)/shard_map/all_to_all | solution.py:19
  22.3 0.7 copy-start.1
  23.0 0.7 copy-start

commit v2 on v1

v2 whole, which is shorter than its diff:
```python
import jax
import jax.numpy as jnp
from jax import lax
from jax.sharding import PartitionSpec as P

SUBS = 64
Y, Z, CORES = 8, 4, 2
PLANES = [[(y * Z + z) * CORES + c for y in range(Y) for c in range(CORES)] for z in range(Z)]
COLUMNS = [[(y * Z + z) * CORES + c for z in range(Z)] for y in range(Y) for c in range(CORES)]
TILE = 8


def exchange(value):
    return lax.all_to_all(value, "grp", 0, 0, tiled=True, axis_index_groups=PLANES)


def on_device(grids, table, coefs):
    local_grids, slots, fields, points = grids.shape
    count = local_grids * slots
    peers = Y * CORES
    own = fields // peers
    blocks = grids.reshape(count, peers, own, points).transpose(1, 2, 0, 3)
    blocks = blocks.reshape(peers, own * count, points)
    known = jnp.stack([table.reshape(count), jnp.repeat(coefs, slots)]).astype(jnp.float32)
    known = jnp.pad(known, ((0, TILE - 2), (0, points - count)))
    known = jnp.broadcast_to(known[None], (peers, TILE, points))
    got = exchange(jnp.concatenate([blocks, known], axis=1))
    labels = got[:, own * count, :count].reshape(peers * count).astype(jnp.int32)
    weight = got[:, own * count + 1, :count].reshape(peers * count)
    parts = got[:, : own * count].reshape(peers, own, count, points)
    wanted = jnp.arange(SUBS, dtype=jnp.int32)
    onehot = (labels[None, :] == wanted[:, None]).astype(jnp.float32)
    weighted = onehot * weight[None, :]
    partial = jnp.stack(
        [
            jnp.dot(
                weighted,
                parts[:, j].reshape(peers * count, points),
                precision=lax.Precision.HIGHEST,
                preferred_element_type=jnp.float32,
            )
            for j in range(own)
        ]
    )
    sparse = jnp.sum(lax.all_gather(partial, "grp", axis_index_groups=COLUMNS), axis=0)
    picks = jnp.stack(
        [
            jnp.dot(
                onehot.T,
                sparse[j],
                precision=lax.Precision.HIGHEST,
                preferred_element_type=jnp.float32,
            ).reshape(peers, count, points)
            for j in range(own)
        ],
        axis=1,
    )
    back = exchange(picks.reshape(peers, own * count, points))
    back = back.reshape(fields, count, points).transpose(1, 0, 2)
    return back.reshape(local_grids, slots, fields, points)


def solution(mesh):
    return jax.shard_map(
        on_device,
        mesh=mesh,
        in_specs=(P("grp", None, None, "dom"), P("grp", None), P("grp")),
        out_specs=P("grp", None, None, "dom"),
        check_vma=False,
    )
```

time: 101 us -> 82.8 us (0.82)
  the two profiles are of different devices: /device:TPU:69 before, /device:TPU:1 now
where the time goes in v2:
time: 82.8 us; the launch traced here: 82.5 us
  blocking collectives  76.7 us (93%)
  local copies, waits for them, and re-layouts  3.54 us (4%)
  matrix products  1.9 us (2%)
    all_to_all x2, blocking collectives, exchange(): lax.all_to_all(value, 'grp', 0, 0, tiled=True, axis_index_groups=PLANES)  52.3 us
    all_gather x1, blocking collectives, on_device(): lax.all_gather(partial, 'grp', axis_index_groups=COLUMNS)  24.4 us

profile of v2, /device:TPU:1, one launch (start us, length us, event | category | flops | bytes accessed | tf_op | source)
XLA Modules:
  0.0 82.5 jit_solution(4816477301312419157)
XLA Ops:
  0.0 0.0 copy-start
  0.0 0.8 stack_reshape.4
  0.8 0.0 copy-done
  0.8 0.1 broadcast_in_dim.4
  0.8 0.1 stack_reshape.5
  0.9 1.3 %copy.11 = f32[2,8,64,128]{3,1,0,2:T(8,128)S(1)} copy(f32[2,8,64,128]{3,2,1,0:T(8,128)} %param.3) | data formatting | bytes 1048576 | tf_op args[0]
  2.4 32.0 %all_to_all.10 = f32[16,72,128]{2,1,0:T(8,128)S(1)} all-to-all(f32[16,72,128]{2,1,0:T(8,128)S(1)} %pad_maximum_fusion), channel_id=1, replica_groups={{0,12,96,108,192,204,288,300,384,396,480,492,576,588,672,684},{24,36,12..., dimensions={0} | all-to-all | bytes 1179648 | tf_op jit(solution)/shard_map/all_to_all | solution.py:14
  34.4 0.1 convert_element_type.23
  34.5 0.1 mul.10
  34.7 0.2 convolution_bitcast_fusion.7
  34.9 0.2 convolution_bitcast_fusion.5
  35.2 0.2 convolution_bitcast_fusion.6
  35.4 0.2 convolution_bitcast_fusion.4
  35.6 24.4 %all-gather = f32[16,64,128]{2,1,0:T(8,128)S(1)} all-gather(f32[4,64,128]{2,1,0:T(8,128)S(1)} %pad_maximum_fusion.2), channel_id=2, replica_groups={{0,24,48,72},{12,36,60,84},{96,120,144,168},{108,132,156,180},{192,216,..., dimensions={0}, use_global_device_ids=true | all-gather | bytes 655360 | tf_op jit(solution)/shard_map/all_gather | solution.py:45
  60.1 0.3 convolution_bitcast_fusion
  60.4 0.3 convolution_bitcast_fusion.1
  60.6 0.3 convolution_bitcast_fusion.2
  60.9 0.3 convolution_bitcast_fusion.3
  61.3 20.3 %all_to_all.11 = f32[16,64,128]{2,1,0:T(8,128)S(1)} all-to-all(f32[16,64,128]{2,1,0:T(8,128)S(1)} %bitcast.71), channel_id=1, replica_groups={{0,12,96,108,192,204,288,300,384,396,480,492,576,588,672,684},{24,36,12..., dimensions={0} | all-to-all | bytes 1048576 | tf_op jit(solution)/shard_map/all_to_all | solution.py:14
  81.5 1.0 %copy.17 = f32[2,8,64,128]{3,2,1,0:T(8,128)} copy(f32[2,8,64,128]{3,1,0,2:T(8,128)S(1)} %bitcast.72) | data formatting | bytes 1048576 | tf_op jit(solution)/shard_map/reshape | solution.py:60
  (12 shorter events, 0.3 us)
Async XLA Ops:
  0.0 0.8 copy-start

commit v3 on v1

v3 whole, which is shorter than its diff:
```python
import jax
import jax.numpy as jnp
from jax import lax
from jax.experimental import pallas as pl
from jax.experimental.pallas import tpu as pltpu
from jax.sharding import PartitionSpec as P

SUBS = 64
Y, Z, CORES = 8, 4, 2
PLANES = [[(y * Z + z) * CORES + c for y in range(Y) for c in range(CORES)] for z in range(Z)]
COLUMNS = [[(y * Z + z) * CORES + c for z in range(Z)] for y in range(Y) for c in range(CORES)]
PEERS = Y * CORES
COUNT = 16
FIELDS = 64
POINTS = 128
OWN = FIELDS // PEERS
ROWS = OWN * COUNT
TILE = 8
VMEM = pl.BlockSpec(memory_space=pltpu.VMEM)
ROOM = pltpu.CompilerParams(vmem_limit_bytes=8 << 20)
SMEM = pl.BlockSpec(memory_space=pltpu.SMEM)


def exchange(value):
    return lax.all_to_all(value, "grp", 0, 0, tiled=True, axis_index_groups=PLANES)


def thirds(value):
    high = value.astype(jnp.bfloat16)
    rest = value - high.astype(jnp.float32)
    mid = rest.astype(jnp.bfloat16)
    low = (rest - mid.astype(jnp.float32)).astype(jnp.bfloat16)
    return high, mid, low


def pack_kernel(table_ref, coefs_ref, grids_ref, out_ref):
    slots = table_ref.shape[1]
    lane = lax.broadcasted_iota(jnp.int32, (TILE, POINTS), 1) % COUNT
    row = lax.broadcasted_iota(jnp.int32, (TILE, POINTS), 0)
    known = jnp.zeros((TILE, POINTS), jnp.int32)
    for i in range(COUNT):
        g, k = divmod(i, slots)
        known = jnp.where(lane == i, jnp.where(row == 0, table_ref[g, k], coefs_ref[g]), known)
    known = known.astype(jnp.float32)
    for peer in range(PEERS):
        for j in range(OWN):
            out_ref[peer, j * COUNT : (j + 1) * COUNT, :] = grids_ref[:, peer * OWN + j, :]
        out_ref[peer, ROWS:, :] = known


def in_one_row(rows):
    peer = lax.broadcasted_iota(jnp.int32, rows.shape, 0)
    part = lax.broadcasted_iota(jnp.int32, rows.shape, 1) // COUNT
    per = POINTS // COUNT
    return jnp.concatenate(
        [
            jnp.sum(jnp.where(peer == part + h * per, rows, 0.0), axis=0, keepdims=True)
            for h in range(PEERS // per)
        ],
        axis=1,
    )


def sum_kernel(got_ref, out_ref, labels_ref):
    labels = in_one_row(got_ref[:, ROWS, :])
    weight = in_one_row(got_ref[:, ROWS + 1, :])
    wanted = lax.broadcasted_iota(jnp.int32, (SUBS, PEERS * COUNT), 0).astype(jnp.float32)
    weighted = jnp.where(labels == wanted, weight, 0.0).astype(jnp.bfloat16)
    data = jnp.concatenate(
        [
            got_ref[:, j * COUNT : (j + 1) * COUNT, :].reshape(PEERS * COUNT, POINTS)
            for j in range(OWN)
        ],
        axis=1,
    )
    high, mid, low = (
        jnp.dot(weighted, part, preferred_element_type=jnp.float32) for part in thirds(data)
    )
    total = high + (mid + low)
    for j in range(OWN):
        out_ref[j] = total[:, j * POINTS : (j + 1) * POINTS]
    labels_ref[...] = jnp.broadcast_to(labels, labels_ref.shape)


def pick_kernel(every_ref, labels_ref, out_ref):
    sparse = jnp.concatenate(
        [
            (every_ref[0, j] + every_ref[1, j]) + (every_ref[2, j] + every_ref[3, j])
            for j in range(OWN)
        ],
        axis=1,
    )
    wanted = lax.broadcasted_iota(jnp.int32, (SUBS, PEERS * COUNT), 0).astype(jnp.float32)
    onehot = (labels_ref[0:1, :] == wanted).astype(jnp.float32).T.astype(jnp.bfloat16)
    picks = jnp.dot(
        jnp.concatenate([onehot] * 3, axis=1),
        jnp.concatenate(thirds(sparse), axis=0),
        preferred_element_type=jnp.float32,
    )
    for j in range(OWN):
        out_ref[:, j * COUNT : (j + 1) * COUNT, :] = picks[
            :, j * POINTS : (j + 1) * POINTS
        ].reshape(PEERS, COUNT, POINTS)


def unpack_kernel(back_ref, out_ref):
    for r in range(COUNT):
        for f in range(0, FIELDS, TILE):
            out_ref[r, f : f + TILE, :] = back_ref[f : f + TILE, r, :]


def on_device(grids, table, coefs):
    f32 = jnp.float32
    message = pl.pallas_call(
        pack_kernel,
        out_shape=jax.ShapeDtypeStruct((PEERS, ROWS + TILE, POINTS), f32),
        in_specs=[SMEM, SMEM, VMEM],
        out_specs=VMEM,
        compiler_params=ROOM,
    )(table, coefs, grids.reshape(COUNT, FIELDS, POINTS))
    partial, labels = pl.pallas_call(
        sum_kernel,
        out_shape=(
            jax.ShapeDtypeStruct((OWN, SUBS, POINTS), f32),
            jax.ShapeDtypeStruct((TILE, PEERS * COUNT), f32),
        ),
        in_specs=[VMEM],
        out_specs=(VMEM, VMEM),
        compiler_params=ROOM,
    )(exchange(message))
    every = lax.all_gather(partial, "grp", axis_index_groups=COLUMNS)
    picks = pl.pallas_call(
        pick_kernel,
        out_shape=jax.ShapeDtypeStruct((PEERS, ROWS, POINTS), f32),
        in_specs=[VMEM, VMEM],
        out_specs=VMEM,
        compiler_params=ROOM,
    )(every, labels)
    back = exchange(picks).reshape(FIELDS, COUNT, POINTS)
    combined = pl.pallas_call(
        unpack_kernel,
        out_shape=jax.ShapeDtypeStruct((COUNT, FIELDS, POINTS), f32),
        in_specs=[VMEM],
        out_specs=VMEM,
        compiler_params=ROOM,
    )(back)
    return combined.reshape(grids.shape)


def solution(mesh):
    return jax.shard_map(
        on_device,
        mesh=mesh,
        in_specs=(P("grp", None, None, "dom"), P("grp", None), P("grp")),
        out_specs=P("grp", None, None, "dom"),
        check_vma=False,
    )
```

time: 101 us -> 81.4 us (0.81)
  the two profiles are of different devices: /device:TPU:69 before, /device:TPU:1 now
where the time goes in v3:
time: 81.4 us; the launch traced here: 81.1 us
  blocking collectives  76.7 us (94%)
  Pallas kernels  2.64 us (3%)
  local copies, waits for them, and re-layouts  1.73 us (2%)
    all_to_all x2, blocking collectives, exchange(): lax.all_to_all(value, 'grp', 0, 0, tiled=True, axis_index_groups=PLANES)  52.3 us
    all_gather x1, blocking collectives, on_device(): every = lax.all_gather(partial, 'grp', axis_index_groups=COLUMNS)  24.4 us
    unnamed x6, local copies, waits for them, and re-layouts  1.73 us

profile of v3, /device:TPU:1, one launch (start us, length us, event | category | flops | bytes accessed | tf_op | source)
XLA Modules:
  0.0 81.1 jit_solution(5508762715384117765)
XLA Ops:
  0.0 0.0 copy-start.2
  0.0 0.0 copy-start.1
  0.0 0.7 copy-done.2
  0.7 0.0 copy-done.1
  0.7 0.0 copy-start
  0.7 1.0 %copy-done = f32[2,8,64,128]{3,2,1,0:T(8,128)S(1)} copy-done((f32[2,8,64,128]{3,2,1,0:T(8,128)S(1)}, f32[2,8,64,128]{3,2,1,0:T(8,128)}, u32[]{:S(2)}) %copy-start) | copy-done | bytes 524312
  1.7 0.8 %shard_map.37 = f32[16,72,128]{2,1,0:T(8,128)S(1)} custom-call(s32[2,8]{1,0:T(2,128)S(1)} %copy-done.1, s32[2]{0:T(128)S(1)} %copy-done.2, f32[16,64,128]{2,1,0:T(8,128)S(1)} %bitcast.6), custom_call_target="tpu_custom_call" | custom-call | tf_op jit(solution)/shard_map/pallas_call | solution.py:114
  2.6 32.0 %all_to_all.10.got_ref = f32[16,72,128]{2,1,0:T(8,128)S(1)} all-to-all(f32[16,72,128]{2,1,0:T(8,128)S(1)} %shard_map.37), channel_id=1, replica_groups={{0,12,96,108,192,204,288,300,384,396,480,492,576,588,672,684},{24,36,12..., dimensions={0} | all-to-all | bytes 1179648 | tf_op jit(solution)/shard_map/all_to_all | solution.py:25
  34.6 0.3 shard_map.38
  34.9 24.4 %all-gather = f32[16,64,128]{2,1,0:T(8,128)S(1)} all-gather(f32[4,64,128]{2,1,0:T(8,128)S(1)} %get-tuple-element.7), channel_id=2, replica_groups={{0,24,48,72},{12,36,60,84},{96,120,144,168},{108,132,156,180},{192,216,..., dimensions={0}, use_global_device_ids=true | all-gather | bytes 655360 | tf_op jit(solution)/shard_map/all_gather | solution.py:131
  59.4 0.4 shard_map.39
  59.8 20.3 %all_to_all.11 = f32[16,64,128]{2,1,0:T(8,128)S(1)} all-to-all(f32[16,64,128]{2,1,0:T(8,128)S(1)} %shard_map.39), channel_id=1, replica_groups={{0,12,96,108,192,204,288,300,384,396,480,492,576,588,672,684},{24,36,12..., dimensions={0} | all-to-all | bytes 1048576 | tf_op jit(solution)/shard_map/all_to_all | solution.py:25
  80.0 1.1 %shard_map.40 = f32[16,64,128]{2,1,0:T(8,128)} custom-call(f32[64,16,128]{2,1,0:T(8,128)S(1)} %bitcast.5), custom_call_target="tpu_custom_call" | custom-call | tf_op jit(solution)/shard_map/pallas_call | solution.py:140
Async XLA Ops:
  0.0 0.7 copy-start.2
  0.0 0.7 copy-start.1
  0.7 1.0 %copy-start = (f32[2,8,64,128]{3,2,1,0:T(8,128)S(1)}, f32[2,8,64,128]{3,2,1,0:T(8,128)}, u32[]{:S(2)}) copy-start(f32[2,8,64,128]{3,2,1,0:T(8,128)} %param.3) | copy-start | bytes 1572868

commit v4 on v3

--- a/solution.py
+++ b/solution.py
@@ -16,13 +16,18 @@
 OWN = FIELDS // PEERS
 ROWS = OWN * COUNT
 TILE = 8
+CHUNKS = 4
 VMEM = pl.BlockSpec(memory_space=pltpu.VMEM)
 ROOM = pltpu.CompilerParams(vmem_limit_bytes=8 << 20)
-SMEM = pl.BlockSpec(memory_space=pltpu.SMEM)
+HBM = pl.BlockSpec(memory_space=pltpu.HBM)
 
 
 def exchange(value):
     return lax.all_to_all(value, "grp", 0, 0, tiled=True, axis_index_groups=PLANES)
+
+
+def in_hbm(value):
+    return pltpu.with_memory_space_constraint(value, pltpu.HBM)
 
 
 def thirds(value):
@@ -33,19 +38,36 @@
     return high, mid, low
 
 
-def pack_kernel(table_ref, coefs_ref, grids_ref, out_ref):
-    slots = table_ref.shape[1]
+def pack_kernel(table_hbm, coefs_hbm, grids_hbm, out_ref, table, coefs, grids, known_sem, grids_sem):
+    known_copies = [
+        pltpu.make_async_copy(table_hbm, table, known_sem.at[0]),
+        pltpu.make_async_copy(coefs_hbm, coefs, known_sem.at[1]),
+    ]
+    chunk = FIELDS // CHUNKS
+    spans = [pl.ds(i * chunk, chunk) for i in range(CHUNKS)]
+    copies = [
+        pltpu.make_async_copy(grids_hbm.at[:, span, :], grids.at[:, span, :], grids_sem.at[i])
+        for i, span in enumerate(spans)
+    ]
+    for copy in known_copies + copies:
+        copy.start()
+    for copy in known_copies:
+        copy.wait()
+    slots = table.shape[1]
     lane = lax.broadcasted_iota(jnp.int32, (TILE, POINTS), 1) % COUNT
     row = lax.broadcasted_iota(jnp.int32, (TILE, POINTS), 0)
     known = jnp.zeros((TILE, POINTS), jnp.int32)
     for i in range(COUNT):
         g, k = divmod(i, slots)
-        known = jnp.where(lane == i, jnp.where(row == 0, table_ref[g, k], coefs_ref[g]), known)
+        known = jnp.where(lane == i, jnp.where(row == 0, table[g, k], coefs[g]), known)
     known = known.astype(jnp.float32)
     for peer in range(PEERS):
-        for j in range(OWN):
-            out_ref[peer, j * COUNT : (j + 1) * COUNT, :] = grids_ref[:, peer * OWN + j, :]
         out_ref[peer, ROWS:, :] = known
+    for i, copy in enumerate(copies):
+        copy.wait()
+        for f in range(i * chunk, (i + 1) * chunk):
+            peer, j = divmod(f, OWN)
+            out_ref[peer, j * COUNT : (j + 1) * COUNT, :] = grids[:, f, :]
 
 
 def in_one_row(rows):
@@ -103,10 +125,18 @@
         ].reshape(PEERS, COUNT, POINTS)
 
 
-def unpack_kernel(back_ref, out_ref):
-    for r in range(COUNT):
-        for f in range(0, FIELDS, TILE):
-            out_ref[r, f : f + TILE, :] = back_ref[f : f + TILE, r, :]
+def unpack_kernel(back_ref, out_hbm, held, sem):
+    chunk = COUNT // CHUNKS
+    copies = []
+    for i in range(CHUNKS):
+        for r in range(i * chunk, (i + 1) * chunk):
+            for f in range(0, FIELDS, TILE):
+                held[r, f : f + TILE, :] = back_ref[f : f + TILE, r, :]
+        span = pl.ds(i * chunk, chunk)
+        copies.append(pltpu.make_async_copy(held.at[span], out_hbm.at[span], sem.at[i]))
+        copies[-1].start()
+    for copy in copies:
+        copy.wait()
 
 
 def on_device(grids, table, coefs):
@@ -114,10 +144,17 @@
     message = pl.pallas_call(
         pack_kernel,
         out_shape=jax.ShapeDtypeStruct((PEERS, ROWS + TILE, POINTS), f32),
-        in_specs=[SMEM, SMEM, VMEM],
+        in_specs=[HBM, HBM, HBM],
         out_specs=VMEM,
+        scratch_shapes=[
+            pltpu.SMEM(table.shape, table.dtype),
+            pltpu.SMEM(coefs.shape, coefs.dtype),
+            pltpu.VMEM((COUNT, FIELDS, POINTS), f32),
+            pltpu.SemaphoreType.DMA((2,)),
+            pltpu.SemaphoreType.DMA((CHUNKS,)),
+        ],
         compiler_params=ROOM,
-    )(table, coefs, grids.reshape(COUNT, FIELDS, POINTS))
+    )(*map(in_hbm, (table, coefs, grids.reshape(COUNT, FIELDS, POINTS))))
     partial, labels = pl.pallas_call(
         sum_kernel,
         out_shape=(
@@ -141,7 +178,11 @@
         unpack_kernel,
         out_shape=jax.ShapeDtypeStruct((COUNT, FIELDS, POINTS), f32),
         in_specs=[VMEM],
-        out_specs=VMEM,
+        out_specs=HBM,
+        scratch_shapes=[
+            pltpu.VMEM((COUNT, FIELDS, POINTS), f32),
+            pltpu.SemaphoreType.DMA((CHUNKS,)),
+        ],
         compiler_params=ROOM,
     )(back)
     return combined.reshape(grids.shape)

time: 81.4 us -> 80 us (0.983)
  local copies, waits for them, and re-layouts: 1.73 us -> 0 us
    unnamed x6 -> x0, local copies, waits for them, and re-layouts: 1.73 us -> none
where the time goes in v4:
time: 80 us; the launch traced here: 79.8 us
  blocking collectives  76.8 us (96%)
  Pallas kernels  2.95 us (4%)
    all_to_all x2, blocking collectives, exchange(): lax.all_to_all(value, 'grp', 0, 0, tiled=True, axis_index_groups=PLANES)  52.4 us
    all_gather x1, blocking collectives, on_device(): every = lax.all_gather(partial, 'grp', axis_index_groups=COLUMNS)  24.4 us

profile of v4, /device:TPU:1, one launch (start us, length us, event | category | flops | bytes accessed | tf_op | source)
XLA Modules:
  0.0 79.8 jit_solution(11864701964914907350)
XLA Ops:
  0.0 1.3 %shard_map.37 = f32[16,72,128]{2,1,0:T(8,128)S(1)} custom-call(s32[2,8]{1,0:T(2,128)} %table_hbm.1, s32[2]{0:T(128)} %coefs_hbm.1, f32[16,64,128]{2,1,0:T(8,128)} %bitcast.6), custom_call_target="tpu_custom_call" | custom-call | tf_op jit(solution)/shard_map/pallas_call | solution.py:144
  1.3 32.0 %all_to_all.10.got_ref = f32[16,72,128]{2,1,0:T(8,128)S(1)} all-to-all(f32[16,72,128]{2,1,0:T(8,128)S(1)} %shard_map.37), channel_id=1, replica_groups={{0,12,96,108,192,204,288,300,384,396,480,492,576,588,672,684},{24,36,12..., dimensions={0} | all-to-all | bytes 1179648 | tf_op jit(solution)/shard_map/all_to_all | solution.py:26
  33.3 0.3 shard_map.38
  33.6 24.4 %all-gather = f32[16,64,128]{2,1,0:T(8,128)S(1)} all-gather(f32[4,64,128]{2,1,0:T(8,128)S(1)} %get-tuple-element.7), channel_id=2, replica_groups={{0,24,48,72},{12,36,60,84},{96,120,144,168},{108,132,156,180},{192,216,..., dimensions={0}, use_global_device_ids=true | all-gather | bytes 655360 | tf_op jit(solution)/shard_map/all_gather | solution.py:168
  58.0 0.4 shard_map.39
  58.5 20.4 %all_to_all.11 = f32[16,64,128]{2,1,0:T(8,128)S(1)} all-to-all(f32[16,64,128]{2,1,0:T(8,128)S(1)} %shard_map.39), channel_id=1, replica_groups={{0,12,96,108,192,204,288,300,384,396,480,492,576,588,672,684},{24,36,12..., dimensions={0} | all-to-all | bytes 1048576 | tf_op jit(solution)/shard_map/all_to_all | solution.py:26
  78.8 1.0 %shard_map.40 = f32[16,64,128]{2,1,0:T(8,128)} custom-call(f32[64,16,128]{2,1,0:T(8,128)S(1)} %bitcast.5), custom_call_target="tpu_custom_call" | custom-call | tf_op jit(solution)/shard_map/pallas_call | solution.py:177

commit v5 on v4

v5 whole, which is shorter than its diff:
```python
import jax
import jax.numpy as jnp
from jax import lax
from jax.experimental import pallas as pl
from jax.experimental.pallas import tpu as pltpu
from jax.sharding import PartitionSpec as P

SUBS = 64
COUNT = 16
FIELDS = 64
POINTS = 128
PEERS = 64
ROWS = COUNT + 1
TILE = 8
CHUNKS = 4
VMEM = pl.BlockSpec(memory_space=pltpu.VMEM)
ROOM = pltpu.CompilerParams(vmem_limit_bytes=8 << 20)
HBM = pl.BlockSpec(memory_space=pltpu.HBM)


def in_hbm(value):
    return pltpu.with_memory_space_constraint(value, pltpu.HBM)


def thirds(value):
    high = value.astype(jnp.bfloat16)
    rest = value - high.astype(jnp.float32)
    mid = rest.astype(jnp.bfloat16)
    low = (rest - mid.astype(jnp.float32)).astype(jnp.bfloat16)
    return high, mid, low


def pack_kernel(table_hbm, coefs_hbm, grids_hbm, out_ref, table, coefs, grids, known_sem, grids_sem):
    known_copies = [
        pltpu.make_async_copy(table_hbm, table, known_sem.at[0]),
        pltpu.make_async_copy(coefs_hbm, coefs, known_sem.at[1]),
    ]
    chunk = FIELDS // CHUNKS
    spans = [pl.ds(i * chunk, chunk) for i in range(CHUNKS)]
    copies = [
        pltpu.make_async_copy(grids_hbm.at[:, span, :], grids.at[:, span, :], grids_sem.at[i])
        for i, span in enumerate(spans)
    ]
    for copy in known_copies + copies:
        copy.start()
    for copy in known_copies:
        copy.wait()
    slots = table.shape[1]
    lane = lax.broadcasted_iota(jnp.int32, (1, POINTS), 1) % COUNT
    labels = jnp.zeros((1, POINTS), jnp.int32)
    for i in range(COUNT):
        labels = jnp.where(lane == i, table[i // slots, i % slots], labels)
    labels = labels.astype(jnp.float32)
    row = lax.broadcasted_iota(jnp.int32, (COUNT, POINTS), 0)
    weight = jnp.zeros((COUNT, POINTS), jnp.int32)
    for g in range(COUNT // slots):
        weight = jnp.where(row // slots == g, coefs[g], weight)
    weight = weight.astype(jnp.float32)
    for i, copy in enumerate(copies):
        copy.wait()
        for f in range(i * chunk, (i + 1) * chunk):
            out_ref[f * ROWS : f * ROWS + COUNT, :] = grids[:, f, :] * weight
            out_ref[f * ROWS + COUNT : (f + 1) * ROWS, :] = labels


def in_one_row(rows):
    per = POINTS // COUNT
    peer = lax.broadcasted_iota(jnp.int32, (per, POINTS), 0)
    part = lax.broadcasted_iota(jnp.int32, (per, POINTS), 1) // COUNT
    return jnp.concatenate(
        [
            jnp.sum(jnp.where(peer == part, rows[s : s + per], 0.0), axis=0, keepdims=True)
            for s in range(0, PEERS, per)
        ],
        axis=1,
    )


def sum_kernel(got_ref, out_ref):
    labels = in_one_row(
        jnp.concatenate(
            [got_ref[s * ROWS + COUNT : (s + 1) * ROWS, :] for s in range(PEERS)], axis=0
        )
    )
    wanted = lax.broadcasted_iota(jnp.int32, (SUBS, PEERS * COUNT), 0).astype(jnp.float32)
    onehot = (labels == wanted).astype(jnp.float32)
    data = jnp.concatenate(
        [got_ref[s * ROWS : s * ROWS + COUNT, :] for s in range(PEERS)], axis=0
    )
    total = jnp.dot(
        onehot.astype(jnp.bfloat16),
        jnp.concatenate(thirds(data), axis=1),
        preferred_element_type=jnp.float32,
    )
    sparse = total[:, :POINTS] + (
        total[:, POINTS : 2 * POINTS] + total[:, 2 * POINTS :]
    )
    turned = onehot.T.astype(jnp.bfloat16)
    out_ref[...] = jnp.dot(
        jnp.concatenate([turned] * 3, axis=1),
        jnp.concatenate(thirds(sparse), axis=0),
        preferred_element_type=jnp.float32,
    )


def unpack_kernel(back_ref, out_hbm, held, sem):
    chunk = COUNT // CHUNKS
    copies = []
    for i in range(CHUNKS):
        for r in range(i * chunk, (i + 1) * chunk):
            for f in range(0, FIELDS, TILE):
                held[r, f : f + TILE, :] = back_ref[f : f + TILE, r, :]
        span = pl.ds(i * chunk, chunk)
        copies.append(pltpu.make_async_copy(held.at[span], out_hbm.at[span], sem.at[i]))
        copies[-1].start()
    for copy in copies:
        copy.wait()


def on_device(grids, table, coefs):
    f32 = jnp.float32
    messages = pl.pallas_call(
        pack_kernel,
        out_shape=jax.ShapeDtypeStruct((PEERS * ROWS, POINTS), f32),
        in_specs=[HBM, HBM, HBM],
        out_specs=VMEM,
        scratch_shapes=[
            pltpu.SMEM(table.shape, table.dtype),
            pltpu.SMEM(coefs.shape, coefs.dtype),
            pltpu.VMEM((COUNT, FIELDS, POINTS), f32),
            pltpu.SemaphoreType.DMA((2,)),
            pltpu.SemaphoreType.DMA((CHUNKS,)),
        ],
        compiler_params=ROOM,
    )(*map(in_hbm, (table, coefs, grids.reshape(COUNT, FIELDS, POINTS))))
    got = lax.all_to_all(messages.reshape(PEERS, 1, ROWS * POINTS), "grp", 0, 0, tiled=True)
    picks = pl.pallas_call(
        sum_kernel,
        out_shape=jax.ShapeDtypeStruct((PEERS * COUNT, POINTS), f32),
        in_specs=[VMEM],
        out_specs=VMEM,
        compiler_params=ROOM,
    )(got.reshape(PEERS * ROWS, POINTS))
    back = lax.all_to_all(picks.reshape(PEERS, COUNT, POINTS), "grp", 0, 0, tiled=True)
    combined = pl.pallas_call(
        unpack_kernel,
        out_shape=jax.ShapeDtypeStruct((COUNT, FIELDS, POINTS), f32),
        in_specs=[VMEM],
        out_specs=HBM,
        scratch_shapes=[
            pltpu.VMEM((COUNT, FIELDS, POINTS), f32),
            pltpu.SemaphoreType.DMA((CHUNKS,)),
        ],
        compiler_params=ROOM,
    )(back)
    return combined.reshape(grids.shape)


def solution(mesh):
    return jax.shard_map(
        on_device,
        mesh=mesh,
        in_specs=(P("grp", None, None, "dom"), P("grp", None), P("grp")),
        out_specs=P("grp", None, None, "dom"),
        check_vma=False,
    )
```

time: 80 us -> 84 us (1.050)
  the two profiles are of different devices: /device:TPU:1 before, /device:TPU:70 now
where the time goes in v5:
time: 84 us; the launch traced here: 83.8 us
  blocking collectives  80.9 us (96%)
  Pallas kernels  2.96 us (4%)
    all_to_all x1, blocking collectives, on_device(): lax.all_to_all(messages.reshape(PEERS, 1, ROWS * POINTS), 'grp', 0, 0, ti...  49.1 us
    all_to_all x1, blocking collectives, on_device(): lax.all_to_all(picks.reshape(PEERS, COUNT, POINTS), 'grp', 0, 0, tiled=True)  31.8 us

profile of v5, /device:TPU:70, one launch (start us, length us, event | category | flops | bytes accessed | tf_op | source)
XLA Modules:
  0.0 83.8 jit_solution(3038207325244310900)
XLA Ops:
  0.0 1.3 %shard_map.37 = f32[1088,128]{1,0:T(8,128)S(1)} custom-call(s32[2,8]{1,0:T(2,128)} %table_hbm.1, s32[2]{0:T(128)} %coefs_hbm.1, f32[16,64,128]{2,1,0:T(8,128)} %bitcast.8), custom_call_target="tpu_custom_call" | custom-call | tf_op jit(solution)/shard_map/pallas_call | solution.py:122
  1.3 49.1 %all_to_all.10 = f32[64,1,2176]{2,1,0:T(1,128)S(1)} all-to-all(f32[64,1,2176]{2,1,0:T(1,128)S(1)} %bitcast.6), channel_id=1, replica_groups=mesh['grp'=64,'dom'=12] {'grp'}, dimensions={0} | all-to-all | bytes 1114112 | tf_op jit(solution)/shard_map/all_to_all | solution.py:136
  50.4 0.7 shard_map.38
  51.1 31.8 %all_to_all.11.back_ref = f32[64,16,128]{2,1,0:T(8,128)S(1)} all-to-all(f32[64,16,128]{2,1,0:T(8,128)S(1)} %bitcast.7), channel_id=1, replica_groups=mesh['grp'=64,'dom'=12] {'grp'}, dimensions={0} | all-to-all | bytes 1048576 | tf_op jit(solution)/shard_map/all_to_all | solution.py:144
  82.9 1.0 %shard_map.39 = f32[16,64,128]{2,1,0:T(8,128)} custom-call(f32[64,16,128]{2,1,0:T(8,128)S(1)} %all_to_all.11.back_ref), custom_call_target="tpu_custom_call" | custom-call | tf_op jit(solution)/shard_map/pallas_call | solution.py:145

commit v6 on v4

--- a/solution.py
+++ b/solution.py
@@ -15,6 +15,7 @@
 POINTS = 128
 OWN = FIELDS // PEERS
 ROWS = OWN * COUNT
+MESSAGE = ROWS + 1
 TILE = 8
 CHUNKS = 4
 VMEM = pl.BlockSpec(memory_space=pltpu.VMEM)
@@ -54,20 +55,24 @@
     for copy in known_copies:
         copy.wait()
     slots = table.shape[1]
-    lane = lax.broadcasted_iota(jnp.int32, (TILE, POINTS), 1) % COUNT
-    row = lax.broadcasted_iota(jnp.int32, (TILE, POINTS), 0)
-    known = jnp.zeros((TILE, POINTS), jnp.int32)
+    lane = lax.broadcasted_iota(jnp.int32, (1, POINTS), 1) % COUNT
+    labels = jnp.zeros((1, POINTS), jnp.int32)
     for i in range(COUNT):
-        g, k = divmod(i, slots)
-        known = jnp.where(lane == i, jnp.where(row == 0, table[g, k], coefs[g]), known)
-    known = known.astype(jnp.float32)
+        labels = jnp.where(lane == i, table[i // slots, i % slots], labels)
+    labels = labels.astype(jnp.float32)
+    row = lax.broadcasted_iota(jnp.int32, (COUNT, POINTS), 0)
+    weight = jnp.zeros((COUNT, POINTS), jnp.int32)
+    for g in range(COUNT // slots):
+        weight = jnp.where(row // slots == g, coefs[g], weight)
+    weight = weight.astype(jnp.float32)
     for peer in range(PEERS):
-        out_ref[peer, ROWS:, :] = known
+        out_ref[peer * MESSAGE + ROWS : (peer + 1) * MESSAGE, :] = labels
     for i, copy in enumerate(copies):
         copy.wait()
         for f in range(i * chunk, (i + 1) * chunk):
             peer, j = divmod(f, OWN)
-            out_ref[peer, j * COUNT : (j + 1) * COUNT, :] = grids[:, f, :]
+            at = peer * MESSAGE + j * COUNT
+            out_ref[at : at + COUNT, :] = grids[:, f, :] * weight
 
 
 def in_one_row(rows):
@@ -84,19 +89,27 @@
 
 
 def sum_kernel(got_ref, out_ref, labels_ref):
-    labels = in_one_row(got_ref[:, ROWS, :])
-    weight = in_one_row(got_ref[:, ROWS + 1, :])
+    labels = in_one_row(
+        jnp.concatenate(
+            [got_ref[(s + 1) * MESSAGE - 1 : (s + 1) * MESSAGE, :] for s in range(PEERS)], axis=0
+        )
+    )
     wanted = lax.broadcasted_iota(jnp.int32, (SUBS, PEERS * COUNT), 0).astype(jnp.float32)
-    weighted = jnp.where(labels == wanted, weight, 0.0).astype(jnp.bfloat16)
+    onehot = (labels == wanted).astype(jnp.float32).astype(jnp.bfloat16)
+
+    def rows_of(s, j):
+        at = s * MESSAGE + j * COUNT
+        return got_ref[at : at + COUNT, :]
+
     data = jnp.concatenate(
         [
-            got_ref[:, j * COUNT : (j + 1) * COUNT, :].reshape(PEERS * COUNT, POINTS)
+            jnp.concatenate([rows_of(s, j) for s in range(PEERS)], axis=0)
             for j in range(OWN)
         ],
         axis=1,
     )
     high, mid, low = (
-        jnp.dot(weighted, part, preferred_element_type=jnp.float32) for part in thirds(data)
+        jnp.dot(onehot, part, preferred_element_type=jnp.float32) for part in thirds(data)
     )
     total = high + (mid + low)
     for j in range(OWN):
@@ -141,9 +154,9 @@
 
 def on_device(grids, table, coefs):
     f32 = jnp.float32
-    message = pl.pallas_call(
+    messages = pl.pallas_call(
         pack_kernel,
-        out_shape=jax.ShapeDtypeStruct((PEERS, ROWS + TILE, POINTS), f32),
+        out_shape=jax.ShapeDtypeStruct((PEERS * MESSAGE, POINTS), f32),
         in_specs=[HBM, HBM, HBM],
         out_specs=VMEM,
         scratch_shapes=[
@@ -155,6 +168,7 @@
         ],
         compiler_params=ROOM,
     )(*map(in_hbm, (table, coefs, grids.reshape(COUNT, FIELDS, POINTS))))
+    got = exchange(messages.reshape(PEERS, 1, MESSAGE * POINTS))
     partial, labels = pl.pallas_call(
         sum_kernel,
         out_shape=(
@@ -164,7 +178,7 @@
         in_specs=[VMEM],
         out_specs=(VMEM, VMEM),
         compiler_params=ROOM,
-    )(exchange(message))
+    )(got.reshape(PEERS * MESSAGE, POINTS))
     every = lax.all_gather(partial, "grp", axis_index_groups=COLUMNS)
     picks = pl.pallas_call(
         pick_kernel,

time: 80 us -> 79.9 us (level)
  no operation moved by 1% of the time
where the time goes in v6:
time: 79.9 us; the launch traced here: 79.7 us
  blocking collectives  76.7 us (96%)
  Pallas kernels  2.94 us (4%)
    all_to_all x2, blocking collectives, exchange(): lax.all_to_all(value, 'grp', 0, 0, tiled=True, axis_index_groups=PLANES)  52.5 us
    all_gather x1, blocking collectives, on_device(): every = lax.all_gather(partial, 'grp', axis_index_groups=COLUMNS)  24.2 us

profile of v6, /device:TPU:1, one launch (start us, length us, event | category | flops | bytes accessed | tf_op | source)
XLA Modules:
  0.0 79.7 jit_solution(6607299935549877147)
XLA Ops:
  0.0 1.3 %shard_map.37 = f32[1040,128]{1,0:T(8,128)S(1)} custom-call(s32[2,8]{1,0:T(2,128)} %table_hbm.1, s32[2]{0:T(128)} %coefs_hbm.1, f32[16,64,128]{2,1,0:T(8,128)} %bitcast.10), custom_call_target="tpu_custom_call" | custom-call | tf_op jit(solution)/shard_map/pallas_call | solution.py:157
  1.3 30.8 %all_to_all.10 = f32[16,1,8320]{2,1,0:T(1,128)S(1)} all-to-all(f32[16,1,8320]{2,1,0:T(1,128)S(1)} %bitcast.7), channel_id=1, replica_groups={{0,12,96,108,192,204,288,300,384,396,480,492,576,588,672,684},{24,36,12..., dimensions={0} | all-to-all | bytes 1064960 | tf_op jit(solution)/shard_map/all_to_all | solution.py:27
  32.1 0.3 shard_map.38
  32.4 24.2 %all-gather = f32[16,64,128]{2,1,0:T(8,128)S(1)} all-gather(f32[4,64,128]{2,1,0:T(8,128)S(1)} %get-tuple-element.7), channel_id=2, replica_groups={{0,24,48,72},{12,36,60,84},{96,120,144,168},{108,132,156,180},{192,216,..., dimensions={0}, use_global_device_ids=true | all-gather | bytes 655360 | tf_op jit(solution)/shard_map/all_gather | solution.py:182
  56.6 0.4 shard_map.39
  57.0 21.7 %all_to_all.11 = f32[16,64,128]{2,1,0:T(8,128)S(1)} all-to-all(f32[16,64,128]{2,1,0:T(8,128)S(1)} %shard_map.39), channel_id=1, replica_groups={{0,12,96,108,192,204,288,300,384,396,480,492,576,588,672,684},{24,36,12..., dimensions={0} | all-to-all | bytes 1048576 | tf_op jit(solution)/shard_map/all_to_all | solution.py:27
  78.7 1.0 %shard_map.40 = f32[16,64,128]{2,1,0:T(8,128)} custom-call(f32[64,16,128]{2,1,0:T(8,128)S(1)} %bitcast.9), custom_call_target="tpu_custom_call" | custom-call | tf_op jit(solution)/shard_map/pallas_call | solution.py:191

commit v7 on v6

--- a/solution.py
+++ b/solution.py
@@ -8,6 +8,8 @@
 SUBS = 64
 Y, Z, CORES = 8, 4, 2
 PLANES = [[(y * Z + z) * CORES + c for y in range(Y) for c in range(CORES)] for z in range(Z)]
+LINES = [[(y * Z + z) * CORES + c for y in range(Y)] for z in range(Z) for c in range(CORES)]
+SIBLINGS = [(i, i ^ 1) for i in range(Y * Z * CORES)]
 COLUMNS = [[(y * Z + z) * CORES + c for z in range(Z)] for y in range(Y) for c in range(CORES)]
 PEERS = Y * CORES
 COUNT = 16
@@ -15,7 +17,8 @@
 POINTS = 128
 OWN = FIELDS // PEERS
 ROWS = OWN * COUNT
-MESSAGE = ROWS + 1
+BOTH = CORES * OWN
+MESSAGE = BOTH * COUNT + 1
 TILE = 8
 CHUNKS = 4
 VMEM = pl.BlockSpec(memory_space=pltpu.VMEM)
@@ -23,8 +26,8 @@
 HBM = pl.BlockSpec(memory_space=pltpu.HBM)
 
 
-def exchange(value):
-    return lax.all_to_all(value, "grp", 0, 0, tiled=True, axis_index_groups=PLANES)
+def exchange(value, groups):
+    return lax.all_to_all(value, "grp", 0, 0, tiled=True, axis_index_groups=groups)
 
 
 def in_hbm(value):
@@ -65,36 +68,25 @@
     for g in range(COUNT // slots):
         weight = jnp.where(row // slots == g, coefs[g], weight)
     weight = weight.astype(jnp.float32)
-    for peer in range(PEERS):
-        out_ref[peer * MESSAGE + ROWS : (peer + 1) * MESSAGE, :] = labels
+    for peer in range(Y):
+        out_ref[(peer + 1) * MESSAGE - 1 : (peer + 1) * MESSAGE, :] = labels
     for i, copy in enumerate(copies):
         copy.wait()
         for f in range(i * chunk, (i + 1) * chunk):
-            peer, j = divmod(f, OWN)
+            peer, j = divmod(f, BOTH)
             at = peer * MESSAGE + j * COUNT
             out_ref[at : at + COUNT, :] = grids[:, f, :] * weight
 
 
-def in_one_row(rows):
+def sum_kernel(got_ref, mine_ref, theirs_ref, labels_ref):
+    first_core = lax.axis_index("grp") % CORES == 0
+    rows = jnp.concatenate(
+        [got_ref[(s + 1) * MESSAGE - 1 : (s + 1) * MESSAGE, :] for s in range(Y)], axis=0
+    )
     peer = lax.broadcasted_iota(jnp.int32, rows.shape, 0)
     part = lax.broadcasted_iota(jnp.int32, rows.shape, 1) // COUNT
-    per = POINTS // COUNT
-    return jnp.concatenate(
-        [
-            jnp.sum(jnp.where(peer == part + h * per, rows, 0.0), axis=0, keepdims=True)
-            for h in range(PEERS // per)
-        ],
-        axis=1,
-    )
-
-
-def sum_kernel(got_ref, out_ref, labels_ref):
-    labels = in_one_row(
-        jnp.concatenate(
-            [got_ref[(s + 1) * MESSAGE - 1 : (s + 1) * MESSAGE, :] for s in range(PEERS)], axis=0
-        )
-    )
-    wanted = lax.broadcasted_iota(jnp.int32, (SUBS, PEERS * COUNT), 0).astype(jnp.float32)
+    labels = jnp.sum(jnp.where(peer == part, rows, 0.0), axis=0, keepdims=True)
+    wanted = lax.broadcasted_iota(jnp.int32, (SUBS, Y * COUNT), 0).astype(jnp.float32)
     onehot = (labels == wanted).astype(jnp.float32).astype(jnp.bfloat16)
 
     def rows_of(s, j):
@@ -102,40 +94,50 @@
         return got_ref[at : at + COUNT, :]
 
     data = jnp.concatenate(
+        [jnp.concatenate([rows_of(s, j) for s in range(Y)], axis=0) for j in range(BOTH)],
+        axis=1,
+    )
+    high, mid, low = (
+        jnp.dot(onehot, part, preferred_element_type=jnp.float32) for part in thirds(data)
+    )
+    total = high + (mid + low)
+    for j in range(OWN):
+        first = total[:, j * POINTS : (j + 1) * POINTS]
+        second = total[:, (OWN + j) * POINTS : (OWN + j + 1) * POINTS]
+        mine_ref[j * SUBS : (j + 1) * SUBS, :] = jnp.where(first_core, first, second)
+        theirs_ref[j * SUBS : (j + 1) * SUBS, :] = jnp.where(first_core, second, first)
+    labels_ref[...] = jnp.broadcast_to(labels, labels_ref.shape)
+    theirs_ref[OWN * SUBS :, :] = jnp.broadcast_to(labels, (TILE, POINTS))
+
+
+def pick_kernel(every_ref, labels_ref, from_sibling_ref, out_ref):
+    first_core = lax.axis_index("grp") % CORES == 0
+    sparse = jnp.concatenate(
         [
-            jnp.concatenate([rows_of(s, j) for s in range(PEERS)], axis=0)
-            for j in range(OWN)
+            (every_ref[0, part] + every_ref[1, part]) + (every_ref[2, part] + every_ref[3, part])
+            for part in (slice(j * SUBS, (j + 1) * SUBS) for j in range(OWN))
         ],
         axis=1,
     )
-    high, mid, low = (
-        jnp.dot(onehot, part, preferred_element_type=jnp.float32) for part in thirds(data)
-    )
-    total = high + (mid + low)
-    for j in range(OWN):
-        out_ref[j] = total[:, j * POINTS : (j + 1) * POINTS]
-    labels_ref[...] = jnp.broadcast_to(labels, labels_ref.shape)
-
-
-def pick_kernel(every_ref, labels_ref, out_ref):
-    sparse = jnp.concatenate(
-        [
-            (every_ref[0, j] + every_ref[1, j]) + (every_ref[2, j] + every_ref[3, j])
-            for j in range(OWN)
-        ],
-        axis=1,
+    own = labels_ref[0:1, :]
+    sibling = from_sibling_ref[OWN * SUBS : OWN * SUBS + 1, :]
+    labels = jnp.concatenate(
+        [jnp.where(first_core, own, sibling), jnp.where(first_core, sibling, own)], axis=1
     )
     wanted = lax.broadcasted_iota(jnp.int32, (SUBS, PEERS * COUNT), 0).astype(jnp.float32)
-    onehot = (labels_ref[0:1, :] == wanted).astype(jnp.float32).T.astype(jnp.bfloat16)
+    onehot = (labels == wanted).astype(jnp.float32).T.astype(jnp.bfloat16)
     picks = jnp.dot(
         jnp.concatenate([onehot] * 3, axis=1),
         jnp.concatenate(thirds(sparse), axis=0),
         preferred_element_type=jnp.float32,
     )
-    for j in range(OWN):
-        out_ref[:, j * COUNT : (j + 1) * COUNT, :] = picks[
-            :, j * POINTS : (j + 1) * POINTS
-        ].reshape(PEERS, COUNT, POINTS)
+    for c in range(CORES):
+        for y in range(Y):
+            at = (c * Y + y) * COUNT
+            for j in range(OWN):
+                out_ref[y * CORES + c, j * COUNT : (j + 1) * COUNT, :] = picks[
+                    at : at + COUNT, j * POINTS : (j + 1) * POINTS
+                ]
 
 
 def unpack_kernel(back_ref, out_hbm, held, sem):
@@ -156,7 +158,7 @@
     f32 = jnp.float32
     messages = pl.pallas_call(
         pack_kernel,
-        out_shape=jax.ShapeDtypeStruct((PEERS * MESSAGE, POINTS), f32),
+        out_shape=jax.ShapeDtypeStruct((Y * MESSAGE, POINTS), f32),
         in_specs=[HBM, HBM, HBM],
         out_specs=VMEM,
         scratch_shapes=[
@@ -168,26 +170,29 @@
         ],
         compiler_params=ROOM,
     )(*map(in_hbm, (table, coefs, grids.reshape(COUNT, FIELDS, POINTS))))
-    got = exchange(messages.reshape(PEERS, 1, MESSAGE * POINTS))
-    partial, labels = pl.pallas_call(
+    got = exchange(messages.reshape(Y, 1, MESSAGE * POINTS), LINES)
+    mine, theirs, labels = pl.pallas_call(
         sum_kernel,
         out_shape=(
-            jax.ShapeDtypeStruct((OWN, SUBS, POINTS), f32),
-            jax.ShapeDtypeStruct((TILE, PEERS * COUNT), f32),
+            jax.ShapeDtypeStruct((OWN * SUBS, POINTS), f32),
+            jax.ShapeDtypeStruct((OWN * SUBS + TILE, POINTS), f32),
+            jax.ShapeDtypeStruct((TILE, POINTS), f32),
         ),
         in_specs=[VMEM],
-        out_specs=(VMEM, VMEM),
-        compiler_params=ROOM,
-    )(got.reshape(PEERS * MESSAGE, POINTS))
+        out_specs=(VMEM, VMEM, VMEM),
+        compiler_params=ROOM,
+    )(got.reshape(Y * MESSAGE, POINTS))
+    from_sibling = lax.ppermute(theirs, "grp", SIBLINGS)
+    partial = mine + from_sibling[: OWN * SUBS]
     every = lax.all_gather(partial, "grp", axis_index_groups=COLUMNS)
     picks = pl.pallas_call(
         pick_kernel,
         out_shape=jax.ShapeDtypeStruct((PEERS, ROWS, POINTS), f32),
-        in_specs=[VMEM, VMEM],
+        in_specs=[VMEM, VMEM, VMEM],
         out_specs=VMEM,
         compiler_params=ROOM,
-    )(every, labels)
-    back = exchange(picks).reshape(FIELDS, COUNT, POINTS)
+    )(every, labels, from_sibling)
+    back = exchange(picks, PLANES).reshape(FIELDS, COUNT, POINTS)
     combined = pl.pallas_call(
         unpack_kernel,
         out_shape=jax.ShapeDtypeStruct((COUNT, FIELDS, POINTS), f32),

time: 79.9 us -> 82.3 us (1.030)
  starting transfers between devices: 0 us -> 8.48 us
  blocking collectives: 76.7 us -> 68.8 us
  waiting for transfers between devices: 0 us -> 0.97 us
    all_to_all x2, blocking collectives: 52.5 us -> 40 us  [exchange(): lax.all_to_all(value, 'grp', 0, 0, tiled=True, axis_index_groups=groups)]
    ppermute x0 -> x1, starting transfers between devices: none -> 8.48 us  [on_device(): from_sibling = lax.ppermute(theirs, 'grp', SIBLINGS)]
    all_gather x1, blocking collectives: 24.2 us -> 28.8 us  [on_device(): every = lax.all_gather(partial, 'grp', axis_index_groups=COLUMNS)]
    ppermute x0 -> x1, waiting for transfers between devices: none -> 0.97 us  [on_device(): from_sibling = lax.ppermute(theirs, 'grp', SIBLINGS)]
  transfers between devices with their start and end apart: 0 -> 1, of which waited for: 0 -> 1; matrix products, arithmetic and copies ran while one was open for 0% -> 0% of each run, Pallas kernels for 0% -> 0%
where the time goes in v7:
time: 82.3 us; the launch traced here: 81.3 us
  blocking collectives  68.8 us (84%)
  starting transfers between devices  8.48 us (10%)
  Pallas kernels  2.97 us (4%)
  waiting for transfers between devices  0.97 us (1%)
    all_to_all x2, blocking collectives, exchange(): lax.all_to_all(value, 'grp', 0, 0, tiled=True, axis_index_groups=groups)  40 us
    all_gather x1, blocking collectives, on_device(): every = lax.all_gather(partial, 'grp', axis_index_groups=COLUMNS)  28.8 us
    ppermute x1, starting transfers between devices, on_device(): from_sibling = lax.ppermute(theirs, 'grp', SIBLINGS)  8.48 us
  transfers between devices with their start and end apart: 1, of which 1 were waited for; matrix products, arithmetic and copies ran while one was open for 0% of the time, Pallas kernels for 0%

profile of v7, /device:TPU:1, one launch (start us, length us, event | category | flops | bytes accessed | tf_op | source)
XLA Modules:
  0.0 81.3 jit_solution(6062811964343877101)
XLA Ops:
  0.0 1.3 %shard_map.37 = f32[1032,128]{1,0:T(8,128)S(1)} custom-call(s32[2,8]{1,0:T(2,128)} %table_hbm.1, s32[2]{0:T(128)} %coefs_hbm.1, f32[16,64,128]{2,1,0:T(8,128)} %bitcast.10), custom_call_target="tpu_custom_call" | custom-call | tf_op jit(solution)/shard_map/pallas_call | solution.py:159
  1.3 19.7 %all_to_all.10 = f32[8,1,16512]{2,1,0:T(1,128)S(1)} all-to-all(f32[8,1,16512]{2,1,0:T(1,128)S(1)} %bitcast.7), channel_id=1, replica_groups={{0,96,192,288,384,480,576,672},{12,108,204,300,396,492,588,684},{24,120..., dimensions={0} | all-to-all | bytes 1056768 | tf_op jit(solution)/shard_map/all_to_all | solution.py:30
  21.0 0.3 shard_map.38
  21.4 8.5 %collective-permute-start = (f32[264,128]{1,0:T(8,128)S(1)}, f32[264,128]{1,0:T(8,128)S(1)}, u32[]{:S(2)}, u32[]{:S(2)}) collective-permute-start(f32[264,128]{1,0:T(8,128)S(1)} %get-tuple-element.9), channel_id=1, source_target_pairs={{0,12},{12,0},{24,36},{36,24},{48,60},{60,48},{72,84},{84,72},{96,... | collective-permute-start | bytes 405512 | tf_op jit(solution)/shard_map/ppermute | solution.py:185
  29.8 1.0 %collective-permute-done.from_sibling_ref = f32[264,128]{1,0:T(8,128)S(1)} collective-permute-done((f32[264,128]{1,0:T(8,128)S(1)}, f32[264,128]{1,0:T(8,128)S(1)}, u32[]{:S(2)}, u32[]{:S(2)}) %collective-permute-start) | collective-permute-done | bytes 135200 | tf_op jit(solution)/shard_map/ppermute | solution.py:185
  30.8 28.8 %all-gather = f32[1024,128]{1,0:T(8,128)S(1)} all-gather(f32[256,128]{1,0:T(8,128)S(1)} %slice_add_fusion), channel_id=2, replica_groups={{0,24,48,72},{12,36,60,84},{96,120,144,168},{108,132,156,180},{192,216,..., dimensions={0}, use_global_device_ids=true | all-gather | bytes 655360 | tf_op jit(solution)/shard_map/all_gather | solution.py:187
  59.7 0.4 shard_map.39
  60.1 20.2 %all_to_all.11 = f32[16,64,128]{2,1,0:T(8,128)S(1)} all-to-all(f32[16,64,128]{2,1,0:T(8,128)S(1)} %shard_map.39), channel_id=1, replica_groups={{0,12,96,108,192,204,288,300,384,396,480,492,576,588,672,684},{24,36,12..., dimensions={0} | all-to-all | bytes 1048576 | tf_op jit(solution)/shard_map/all_to_all | solution.py:30
  80.3 1.0 %shard_map.40 = f32[16,64,128]{2,1,0:T(8,128)} custom-call(f32[64,16,128]{2,1,0:T(8,128)S(1)} %bitcast.9), custom_call_target="tpu_custom_call" | custom-call | tf_op jit(solution)/shard_map/pallas_call | solution.py:196
  (1 shorter events, 0.0 us)
Async XLA Ops:
  21.4 9.5 %collective-permute-start = (f32[264,128]{1,0:T(8,128)S(1)}, f32[264,128]{1,0:T(8,128)S(1)}, u32[]{:S(2)}, u32[]{:S(2)}) collective-permute-start(f32[264,128]{1,0:T(8,128)S(1)} %get-tuple-element.9), channel_id=1, source_target_pairs={{0,12},{12,0},{24,36},{36,24},{48,60},{60,48},{72,84},{84,72},{96,... | collective-permute-start | bytes 405512 | tf_op jit(solution)/shard_map/ppermute | solution.py:185

commit v8 on v6

--- a/solution.py
+++ b/solution.py
@@ -8,7 +8,17 @@
 SUBS = 64
 Y, Z, CORES = 8, 4, 2
 PLANES = [[(y * Z + z) * CORES + c for y in range(Y) for c in range(CORES)] for z in range(Z)]
-COLUMNS = [[(y * Z + z) * CORES + c for z in range(Z)] for y in range(Y) for c in range(CORES)]
+
+
+def partners(turn):
+    pairs = []
+    for i in range(Y * Z * CORES):
+        y, z, c = i // (Z * CORES), i // CORES % Z, i % CORES
+        other = z ^ 1 if turn == c else Z - 1 - z
+        pairs.append((i, (y * Z + other) * CORES + c))
+    return pairs
+
+
 PEERS = Y * CORES
 COUNT = 16
 FIELDS = 64
@@ -117,14 +127,8 @@
     labels_ref[...] = jnp.broadcast_to(labels, labels_ref.shape)
 
 
-def pick_kernel(every_ref, labels_ref, out_ref):
-    sparse = jnp.concatenate(
-        [
-            (every_ref[0, j] + every_ref[1, j]) + (every_ref[2, j] + every_ref[3, j])
-            for j in range(OWN)
-        ],
-        axis=1,
-    )
+def pick_kernel(pair_ref, other_pair_ref, labels_ref, out_ref):
+    sparse = jnp.concatenate([pair_ref[j] + other_pair_ref[j] for j in range(OWN)], axis=1)
     wanted = lax.broadcasted_iota(jnp.int32, (SUBS, PEERS * COUNT), 0).astype(jnp.float32)
     onehot = (labels_ref[0:1, :] == wanted).astype(jnp.float32).T.astype(jnp.bfloat16)
     picks = jnp.dot(
@@ -179,14 +183,15 @@
         out_specs=(VMEM, VMEM),
         compiler_params=ROOM,
     )(got.reshape(PEERS * MESSAGE, POINTS))
-    every = lax.all_gather(partial, "grp", axis_index_groups=COLUMNS)
+    pair = partial + lax.ppermute(partial, "grp", partners(0))
+    other_pair = lax.ppermute(pair, "grp", partners(1))
     picks = pl.pallas_call(
         pick_kernel,
         out_shape=jax.ShapeDtypeStruct((PEERS, ROWS, POINTS), f32),
-        in_specs=[VMEM, VMEM],
+        in_specs=[VMEM, VMEM, VMEM],
         out_specs=VMEM,
         compiler_params=ROOM,
-    )(every, labels)
+    )(pair, other_pair, labels)
     back = exchange(picks).reshape(FIELDS, COUNT, POINTS)
     combined = pl.pallas_call(
         unpack_kernel,

time: 79.9 us -> 80 us (level)
  blocking collectives: 76.7 us -> 54 us
  starting transfers between devices: 0 us -> 11.6 us
  waiting for transfers between devices: 0 us -> 11.1 us
    all_gather x1 -> x0, blocking collectives: 24.2 us -> none  [on_device(): every = lax.all_gather(partial, 'grp', axis_index_groups=COLUMNS)]
    ppermute x0 -> x2, starting transfers between devices: none -> 11.6 us  [the longest x1 9.69 us: on_device(): pair = partial + lax.ppermute(partial, 'grp', partners(0))]
    ppermute x0 -> x2, waiting for transfers between devices: none -> 11.1 us  [the longest x1 6.44 us: on_device(): other_pair = lax.ppermute(pair, 'grp', partners(1))]
    all_to_all x2, blocking collectives: 52.5 us -> 54 us  [exchange(): lax.all_to_all(value, 'grp', 0, 0, tiled=True, axis_index_groups=PLANES)]
  transfers between devices with their start and end apart: 0 -> 2, of which waited for: 0 -> 2; matrix products, arithmetic and copies ran while one was open for 0% -> 0% of each run, Pallas kernels for 0% -> 0%
where the time goes in v8:
time: 80 us; the launch traced here: 79.7 us
  blocking collectives  54 us (68%)
  starting transfers between devices  11.6 us (14%)
  waiting for transfers between devices  11.1 us (14%)
  Pallas kernels  2.95 us (4%)
    all_to_all x2, blocking collectives, exchange(): lax.all_to_all(value, 'grp', 0, 0, tiled=True, axis_index_groups=PLANES)  54 us
    ppermute x1, starting transfers between devices, on_device(): pair = partial + lax.ppermute(partial, 'grp', partners(0))  9.69 us
    ppermute x1, waiting for transfers between devices, on_device(): other_pair = lax.ppermute(pair, 'grp', partners(1))  6.44 us
    ppermute x1, waiting for transfers between devices, on_device(): pair = partial + lax.ppermute(partial, 'grp', partners(0))  4.7 us
    ppermute x1, starting transfers between devices, on_device(): other_pair = lax.ppermute(pair, 'grp', partners(1))  1.92 us
  transfers between devices with their start and end apart: 2, of which 2 were waited for; matrix products, arithmetic and copies ran while one was open for 0% of the time, Pallas kernels for 0%

profile of v8, /device:TPU:1, one launch (start us, length us, event | category | flops | bytes accessed | tf_op | source)
XLA Modules:
  0.0 79.7 jit_solution(2956131107045040290)
XLA Ops:
  0.0 1.3 %shard_map.37 = f32[1040,128]{1,0:T(8,128)S(1)} custom-call(s32[2,8]{1,0:T(2,128)} %table_hbm.1, s32[2]{0:T(128)} %coefs_hbm.1, f32[16,64,128]{2,1,0:T(8,128)} %bitcast.8), custom_call_target="tpu_custom_call" | custom-call | tf_op jit(solution)/shard_map/pallas_call | solution.py:161
  1.3 30.8 %all_to_all.10 = f32[16,1,8320]{2,1,0:T(1,128)S(1)} all-to-all(f32[16,1,8320]{2,1,0:T(1,128)S(1)} %bitcast.6), channel_id=1, replica_groups={{0,12,96,108,192,204,288,300,384,396,480,492,576,588,672,684},{24,36,12..., dimensions={0} | all-to-all | bytes 1064960 | tf_op jit(solution)/shard_map/all_to_all | solution.py:37
  32.1 0.3 shard_map.38
  32.4 9.7 %collective-permute-start = (f32[4,64,128]{2,1,0:T(8,128)S(1)}, f32[4,64,128]{2,1,0:T(8,128)S(1)}, u32[]{:S(2)}, u32[]{:S(2)}) collective-permute-start(f32[4,64,128]{2,1,0:T(8,128)S(1)} %get-tuple-element.7), channel_id=1, source_target_pairs={{0,24},{12,84},{24,0},{36,60},{48,72},{60,36},{72,48},{84,12},{96,... | collective-permute-start | bytes 393224 | tf_op jit(solution)/shard_map/ppermute | solution.py:186
  42.1 4.7 %collective-permute-done = f32[4,64,128]{2,1,0:T(8,128)S(1)} collective-permute-done((f32[4,64,128]{2,1,0:T(8,128)S(1)}, f32[4,64,128]{2,1,0:T(8,128)S(1)}, u32[]{:S(2)}, u32[]{:S(2)}) %collective-permute-start) | collective-permute-done | bytes 131104 | tf_op jit(solution)/shard_map/ppermute | solution.py:186
  46.8 1.9 %collective-permute-start.1 = (f32[4,64,128]{2,1,0:T(8,128)S(1)}, f32[4,64,128]{2,1,0:T(8,128)S(1)}, u32[]{:S(2)}, u32[]{:S(2)}) collective-permute-start(f32[4,64,128]{2,1,0:T(8,128)S(1)} %add.3.pair_ref), channel_id=1, source_target_pairs={{0,72},{12,36},{24,48},{36,12},{48,24},{60,84},{72,0},{84,60},{96,... | collective-permute-start | bytes 393224 | tf_op jit(solution)/shard_map/ppermute | solution.py:187
  48.8 6.4 %collective-permute-done.1.other_pair_ref = f32[4,64,128]{2,1,0:T(8,128)S(1)} collective-permute-done((f32[4,64,128]{2,1,0:T(8,128)S(1)}, f32[4,64,128]{2,1,0:T(8,128)S(1)}, u32[]{:S(2)}, u32[]{:S(2)}) %collective-permute-start.1) | collective-permute-done | bytes 131104 | tf_op jit(solution)/shard_map/ppermute | solution.py:187
  55.2 0.4 shard_map.39
  55.6 23.2 %all_to_all.11 = f32[16,64,128]{2,1,0:T(8,128)S(1)} all-to-all(f32[16,64,128]{2,1,0:T(8,128)S(1)} %shard_map.39), channel_id=1, replica_groups={{0,12,96,108,192,204,288,300,384,396,480,492,576,588,672,684},{24,36,12..., dimensions={0} | all-to-all | bytes 1048576 | tf_op jit(solution)/shard_map/all_to_all | solution.py:37
  78.8 1.0 %shard_map.40 = f32[16,64,128]{2,1,0:T(8,128)} custom-call(f32[64,16,128]{2,1,0:T(8,128)S(1)} %bitcast.7), custom_call_target="tpu_custom_call" | custom-call | tf_op jit(solution)/shard_map/pallas_call | solution.py:196
  (1 shorter events, 0.0 us)
Async XLA Ops:
  32.4 14.4 %collective-permute-start = (f32[4,64,128]{2,1,0:T(8,128)S(1)}, f32[4,64,128]{2,1,0:T(8,128)S(1)}, u32[]{:S(2)}, u32[]{:S(2)}) collective-permute-start(f32[4,64,128]{2,1,0:T(8,128)S(1)} %get-tuple-element.7), channel_id=1, source_target_pairs={{0,24},{12,84},{24,0},{36,60},{48,72},{60,36},{72,48},{84,12},{96,... | collective-permute-start | bytes 393224 | tf_op jit(solution)/shard_map/ppermute | solution.py:186
  46.8 8.4 %collective-permute-start.1 = (f32[4,64,128]{2,1,0:T(8,128)S(1)}, f32[4,64,128]{2,1,0:T(8,128)S(1)}, u32[]{:S(2)}, u32[]{:S(2)}) collective-permute-start(f32[4,64,128]{2,1,0:T(8,128)S(1)} %add.3.pair_ref), channel_id=1, source_target_pairs={{0,72},{12,36},{24,48},{36,12},{48,24},{60,84},{72,0},{84,60},{96,... | collective-permute-start | bytes 393224 | tf_op jit(solution)/shard_map/ppermute | solution.py:187

commit v9 on v6

--- a/solution.py
+++ b/solution.py
@@ -8,7 +8,13 @@
 SUBS = 64
 Y, Z, CORES = 8, 4, 2
 PLANES = [[(y * Z + z) * CORES + c for y in range(Y) for c in range(CORES)] for z in range(Z)]
-COLUMNS = [[(y * Z + z) * CORES + c for z in range(Z)] for y in range(Y) for c in range(CORES)]
+
+
+def along_z(step):
+    places = [(y, z, c) for y in range(Y) for z in range(Z) for c in range(CORES)]
+    return [(i, (y * Z + (z + step) % Z) * CORES + c) for i, (y, z, c) in enumerate(places)]
+
+
 PEERS = Y * CORES
 COUNT = 16
 FIELDS = 64
@@ -117,13 +123,9 @@
     labels_ref[...] = jnp.broadcast_to(labels, labels_ref.shape)
 
 
-def pick_kernel(every_ref, labels_ref, out_ref):
+def pick_kernel(own_ref, far_ref, below_ref, above_ref, labels_ref, out_ref):
     sparse = jnp.concatenate(
-        [
-            (every_ref[0, j] + every_ref[1, j]) + (every_ref[2, j] + every_ref[3, j])
-            for j in range(OWN)
-        ],
-        axis=1,
+        [(own_ref[j] + far_ref[j]) + (below_ref[j] + above_ref[j]) for j in range(OWN)], axis=1
     )
     wanted = lax.broadcasted_iota(jnp.int32, (SUBS, PEERS * COUNT), 0).astype(jnp.float32)
     onehot = (labels_ref[0:1, :] == wanted).astype(jnp.float32).T.astype(jnp.bfloat16)
@@ -179,14 +181,14 @@
         out_specs=(VMEM, VMEM),
         compiler_params=ROOM,
     )(got.reshape(PEERS * MESSAGE, POINTS))
-    every = lax.all_gather(partial, "grp", axis_index_groups=COLUMNS)
+    others = [lax.ppermute(partial, "grp", along_z(step)) for step in (2, 1, 3)]
     picks = pl.pallas_call(
         pick_kernel,
         out_shape=jax.ShapeDtypeStruct((PEERS, ROWS, POINTS), f32),
-        in_specs=[VMEM, VMEM],
+        in_specs=[VMEM] * 5,
         out_specs=VMEM,
         compiler_params=ROOM,
-    )(every, labels)
+    )(partial, *others, labels)
     back = exchange(picks).reshape(FIELDS, COUNT, POINTS)
     combined = pl.pallas_call(
         unpack_kernel,

time: 79.9 us -> 85.8 us (1.074)
  the two profiles are of different devices: /device:TPU:1 before, /device:TPU:131 now
where the time goes in v9:
time: 85.8 us; the launch traced here: 85.5 us
  blocking collectives  46.3 us (54%)
  starting transfers between devices  19.5 us (23%)
  waiting for transfers between devices  16.7 us (19%)
  Pallas kernels  2.94 us (3%)
    all_to_all x2, blocking collectives, exchange(): lax.all_to_all(value, 'grp', 0, 0, tiled=True, axis_index_groups=PLANES)  46.3 us
    ppermute x3, starting transfers between devices, on_device(): others = [lax.ppermute(partial, 'grp', along_z(step)) for step in (2, 1, 3)]  19.5 us
    ppermute x3, waiting for transfers between devices, on_device(): others = [lax.ppermute(partial, 'grp', along_z(step)) for step in (2, 1, 3)]  16.7 us
  transfers between devices with their start and end apart: 3, of which 1 were waited for; matrix products, arithmetic and copies ran while one was open for 0% of the time, Pallas kernels for 0%

profile of v9, /device:TPU:131, one launch (start us, length us, event | category | flops | bytes accessed | tf_op | source)
XLA Modules:
  0.0 85.5 jit_solution(6178312035578287918)
XLA Ops:
  0.0 1.3 %shard_map.37 = f32[1040,128]{1,0:T(8,128)S(1)} custom-call(s32[2,8]{1,0:T(2,128)} %table_hbm.1, s32[2]{0:T(128)} %coefs_hbm.1, f32[16,64,128]{2,1,0:T(8,128)} %bitcast.8), custom_call_target="tpu_custom_call" | custom-call | tf_op jit(solution)/shard_map/pallas_call | solution.py:159
  1.3 25.4 %all_to_all.10 = f32[16,1,8320]{2,1,0:T(1,128)S(1)} all-to-all(f32[16,1,8320]{2,1,0:T(1,128)S(1)} %bitcast.6), channel_id=1, replica_groups={{0,12,96,108,192,204,288,300,384,396,480,492,576,588,672,684},{24,36,12..., dimensions={0} | all-to-all | bytes 1064960 | tf_op jit(solution)/shard_map/all_to_all | solution.py:33
  26.7 0.3 shard_map.38
  27.0 12.5 %collective-permute-start.2 = (f32[4,64,128]{2,1,0:T(8,128)S(1)}, f32[4,64,128]{2,1,0:T(8,128)S(1)}, u32[]{:S(2)}, u32[]{:S(2)}) collective-permute-start(f32[4,64,128]{2,1,0:T(8,128)S(1)} %get-tuple-element.7.own_ref), channel_id=1, source_target_pairs={{0,72},{12,84},{24,0},{36,12},{48,24},{60,36},{72,48},{84,60},{96,... | collective-permute-start | bytes 393224 | tf_op jit(solution)/shard_map/ppermute | solution.py:184
  39.5 1.9 %collective-permute-start.1 = (f32[4,64,128]{2,1,0:T(8,128)S(1)}, f32[4,64,128]{2,1,0:T(8,128)S(1)}, u32[]{:S(2)}, u32[]{:S(2)}) collective-permute-start(f32[4,64,128]{2,1,0:T(8,128)S(1)} %get-tuple-element.7.own_ref), channel_id=1, source_target_pairs={{0,24},{12,36},{24,48},{36,60},{48,72},{60,84},{72,0},{84,12},{96,... | collective-permute-start | bytes 393224 | tf_op jit(solution)/shard_map/ppermute | solution.py:184
  41.4 5.1 %collective-permute-start = (f32[4,64,128]{2,1,0:T(8,128)S(1)}, f32[4,64,128]{2,1,0:T(8,128)S(1)}, u32[]{:S(2)}, u32[]{:S(2)}) collective-permute-start(f32[4,64,128]{2,1,0:T(8,128)S(1)} %get-tuple-element.7.own_ref), channel_id=1, source_target_pairs={{0,48},{12,60},{24,72},{36,84},{48,0},{60,12},{72,24},{84,36},{96,... | collective-permute-start | bytes 393224 | tf_op jit(solution)/shard_map/ppermute | solution.py:184
  46.5 0.0 collective-permute-done.2.above_ref
  46.6 16.7 %collective-permute-done.1.below_ref = f32[4,64,128]{2,1,0:T(8,128)S(1)} collective-permute-done((f32[4,64,128]{2,1,0:T(8,128)S(1)}, f32[4,64,128]{2,1,0:T(8,128)S(1)}, u32[]{:S(2)}, u32[]{:S(2)}) %collective-permute-start.1) | collective-permute-done | bytes 131104 | tf_op jit(solution)/shard_map/ppermute | solution.py:184
  63.3 0.0 collective-permute-done.far_ref
  63.3 0.4 shard_map.39
  63.7 20.9 %all_to_all.11 = f32[16,64,128]{2,1,0:T(8,128)S(1)} all-to-all(f32[16,64,128]{2,1,0:T(8,128)S(1)} %shard_map.39), channel_id=1, replica_groups={{0,12,96,108,192,204,288,300,384,396,480,492,576,588,672,684},{24,36,12..., dimensions={0} | all-to-all | bytes 1048576 | tf_op jit(solution)/shard_map/all_to_all | solution.py:33
  84.6 1.0 %shard_map.40 = f32[16,64,128]{2,1,0:T(8,128)} custom-call(f32[64,16,128]{2,1,0:T(8,128)S(1)} %bitcast.7), custom_call_target="tpu_custom_call" | custom-call | tf_op jit(solution)/shard_map/pallas_call | solution.py:193
Async XLA Ops:
  27.0 19.6 %collective-permute-start.2 = (f32[4,64,128]{2,1,0:T(8,128)S(1)}, f32[4,64,128]{2,1,0:T(8,128)S(1)}, u32[]{:S(2)}, u32[]{:S(2)}) collective-permute-start(f32[4,64,128]{2,1,0:T(8,128)S(1)} %get-tuple-element.7.own_ref), channel_id=1, source_target_pairs={{0,72},{12,84},{24,0},{36,12},{48,24},{60,36},{72,48},{84,60},{96,... | collective-permute-start | bytes 393224 | tf_op jit(solution)/shard_map/ppermute | solution.py:184
  39.5 23.8 %collective-permute-start.1 = (f32[4,64,128]{2,1,0:T(8,128)S(1)}, f32[4,64,128]{2,1,0:T(8,128)S(1)}, u32[]{:S(2)}, u32[]{:S(2)}) collective-permute-start(f32[4,64,128]{2,1,0:T(8,128)S(1)} %get-tuple-element.7.own_ref), channel_id=1, source_target_pairs={{0,24},{12,36},{24,48},{36,60},{48,72},{60,84},{72,0},{84,12},{96,... | collective-permute-start | bytes 393224 | tf_op jit(solution)/shard_map/ppermute | solution.py:184
  41.4 21.8 %collective-permute-start = (f32[4,64,128]{2,1,0:T(8,128)S(1)}, f32[4,64,128]{2,1,0:T(8,128)S(1)}, u32[]{:S(2)}, u32[]{:S(2)}) collective-permute-start(f32[4,64,128]{2,1,0:T(8,128)S(1)} %get-tuple-element.7.own_ref), channel_id=1, source_target_pairs={{0,48},{12,60},{24,72},{36,84},{48,0},{60,12},{72,24},{84,36},{96,... | collective-permute-start | bytes 393224 | tf_op jit(solution)/shard_map/ppermute | solution.py:184

commit v10 on v8

--- a/solution.py
+++ b/solution.py
@@ -14,7 +14,7 @@
     pairs = []
     for i in range(Y * Z * CORES):
         y, z, c = i // (Z * CORES), i // CORES % Z, i % CORES
-        other = z ^ 1 if turn == c else Z - 1 - z
+        other = ((z ^ 2, Z - 1 - z), (Z - 1 - z, z ^ 1))[c][turn]
         pairs.append((i, (y * Z + other) * CORES + c))
     return pairs
 

time: 80 us -> 85.6 us (1.070)
  waiting for transfers between devices: 11.1 us -> 14 us
  blocking collectives: 54 us -> 56.8 us
    ppermute x1, waiting for transfers between devices: 4.7 us -> 8.4 us  [on_device(): pair = partial + lax.ppermute(partial, 'grp', partners(0))]
    all_to_all x2, blocking collectives: 54 us -> 56.8 us  [exchange(): lax.all_to_all(value, 'grp', 0, 0, tiled=True, axis_index_groups=PLANES)]
where the time goes in v10:
time: 85.6 us; the launch traced here: 85.4 us
  blocking collectives  56.8 us (66%)
  waiting for transfers between devices  14 us (16%)
  starting transfers between devices  11.6 us (14%)
  Pallas kernels  2.95 us (3%)
    all_to_all x2, blocking collectives, exchange(): lax.all_to_all(value, 'grp', 0, 0, tiled=True, axis_index_groups=PLANES)  56.8 us
    ppermute x1, starting transfers between devices, on_device(): pair = partial + lax.ppermute(partial, 'grp', partners(0))  9.69 us
    ppermute x1, waiting for transfers between devices, on_device(): pair = partial + lax.ppermute(partial, 'grp', partners(0))  8.4 us
    ppermute x1, waiting for transfers between devices, on_device(): other_pair = lax.ppermute(pair, 'grp', partners(1))  5.58 us
    ppermute x1, starting transfers between devices, on_device(): other_pair = lax.ppermute(pair, 'grp', partners(1))  1.92 us
  transfers between devices with their start and end apart: 2, of which 2 were waited for; matrix products, arithmetic and copies ran while one was open for 0% of the time, Pallas kernels for 0%

profile of v10, /device:TPU:1, one launch (start us, length us, event | category | flops | bytes accessed | tf_op | source)
XLA Modules:
  0.0 85.4 jit_solution(12656446170854668573)
XLA Ops:
  0.0 1.3 %shard_map.37 = f32[1040,128]{1,0:T(8,128)S(1)} custom-call(s32[2,8]{1,0:T(2,128)} %table_hbm.1, s32[2]{0:T(128)} %coefs_hbm.1, f32[16,64,128]{2,1,0:T(8,128)} %bitcast.8), custom_call_target="tpu_custom_call" | custom-call | tf_op jit(solution)/shard_map/pallas_call | solution.py:161
  1.3 30.8 %all_to_all.10 = f32[16,1,8320]{2,1,0:T(1,128)S(1)} all-to-all(f32[16,1,8320]{2,1,0:T(1,128)S(1)} %bitcast.6), channel_id=1, replica_groups={{0,12,96,108,192,204,288,300,384,396,480,492,576,588,672,684},{24,36,12..., dimensions={0} | all-to-all | bytes 1064960 | tf_op jit(solution)/shard_map/all_to_all | solution.py:37
  32.1 0.3 shard_map.38
  32.4 9.7 %collective-permute-start = (f32[4,64,128]{2,1,0:T(8,128)S(1)}, f32[4,64,128]{2,1,0:T(8,128)S(1)}, u32[]{:S(2)}, u32[]{:S(2)}) collective-permute-start(f32[4,64,128]{2,1,0:T(8,128)S(1)} %get-tuple-element.7), channel_id=1, source_target_pairs={{0,48},{12,84},{24,72},{36,60},{48,0},{60,36},{72,24},{84,12},{96,... | collective-permute-start | bytes 393224 | tf_op jit(solution)/shard_map/ppermute | solution.py:186
  42.1 8.4 %collective-permute-done = f32[4,64,128]{2,1,0:T(8,128)S(1)} collective-permute-done((f32[4,64,128]{2,1,0:T(8,128)S(1)}, f32[4,64,128]{2,1,0:T(8,128)S(1)}, u32[]{:S(2)}, u32[]{:S(2)}) %collective-permute-start) | collective-permute-done | bytes 131104 | tf_op jit(solution)/shard_map/ppermute | solution.py:186
  50.5 1.9 %collective-permute-start.1 = (f32[4,64,128]{2,1,0:T(8,128)S(1)}, f32[4,64,128]{2,1,0:T(8,128)S(1)}, u32[]{:S(2)}, u32[]{:S(2)}) collective-permute-start(f32[4,64,128]{2,1,0:T(8,128)S(1)} %add.3.pair_ref), channel_id=1, source_target_pairs={{0,72},{12,36},{24,48},{36,12},{48,24},{60,84},{72,0},{84,60},{96,... | collective-permute-start | bytes 393224 | tf_op jit(solution)/shard_map/ppermute | solution.py:187
  52.5 5.6 %collective-permute-done.1.other_pair_ref = f32[4,64,128]{2,1,0:T(8,128)S(1)} collective-permute-done((f32[4,64,128]{2,1,0:T(8,128)S(1)}, f32[4,64,128]{2,1,0:T(8,128)S(1)}, u32[]{:S(2)}, u32[]{:S(2)}) %collective-permute-start.1) | collective-permute-done | bytes 131104 | tf_op jit(solution)/shard_map/ppermute | solution.py:187
  58.0 0.4 shard_map.39
  58.4 25.9 %all_to_all.11 = f32[16,64,128]{2,1,0:T(8,128)S(1)} all-to-all(f32[16,64,128]{2,1,0:T(8,128)S(1)} %shard_map.39), channel_id=1, replica_groups={{0,12,96,108,192,204,288,300,384,396,480,492,576,588,672,684},{24,36,12..., dimensions={0} | all-to-all | bytes 1048576 | tf_op jit(solution)/shard_map/all_to_all | solution.py:37
  84.4 1.0 %shard_map.40 = f32[16,64,128]{2,1,0:T(8,128)} custom-call(f32[64,16,128]{2,1,0:T(8,128)S(1)} %bitcast.7), custom_call_target="tpu_custom_call" | custom-call | tf_op jit(solution)/shard_map/pallas_call | solution.py:196
  (1 shorter events, 0.0 us)
Async XLA Ops:
  32.4 18.1 %collective-permute-start = (f32[4,64,128]{2,1,0:T(8,128)S(1)}, f32[4,64,128]{2,1,0:T(8,128)S(1)}, u32[]{:S(2)}, u32[]{:S(2)}) collective-permute-start(f32[4,64,128]{2,1,0:T(8,128)S(1)} %get-tuple-element.7), channel_id=1, source_target_pairs={{0,48},{12,84},{24,72},{36,60},{48,0},{60,36},{72,24},{84,12},{96,... | collective-permute-start | bytes 393224 | tf_op jit(solution)/shard_map/ppermute | solution.py:186
  50.5 7.5 %collective-permute-start.1 = (f32[4,64,128]{2,1,0:T(8,128)S(1)}, f32[4,64,128]{2,1,0:T(8,128)S(1)}, u32[]{:S(2)}, u32[]{:S(2)}) collective-permute-start(f32[4,64,128]{2,1,0:T(8,128)S(1)} %add.3.pair_ref), channel_id=1, source_target_pairs={{0,72},{12,36},{24,48},{36,12},{48,24},{60,84},{72,0},{84,60},{96,... | collective-permute-start | bytes 393224 | tf_op jit(solution)/shard_map/ppermute | solution.py:187

commit v11 on v10

--- a/solution.py
+++ b/solution.py
@@ -14,7 +14,7 @@
     pairs = []
     for i in range(Y * Z * CORES):
         y, z, c = i // (Z * CORES), i // CORES % Z, i % CORES
-        other = ((z ^ 2, Z - 1 - z), (Z - 1 - z, z ^ 1))[c][turn]
+        other = (Z - 1 - z, z ^ 1)[turn]
         pairs.append((i, (y * Z + other) * CORES + c))
     return pairs
 

time: 85.6 us -> 86.5 us (1.011)
  blocking collectives: 56.8 us -> 55.2 us
  starting transfers between devices: 11.6 us -> 13 us
  waiting for transfers between devices: 14 us -> 15.1 us
    ppermute x1, waiting for transfers between devices: 5.58 us -> 7.38 us  [on_device(): other_pair = lax.ppermute(pair, 'grp', partners(1))]
    all_to_all x2, blocking collectives: 56.8 us -> 55.2 us  [exchange(): lax.all_to_all(value, 'grp', 0, 0, tiled=True, axis_index_groups=PLANES)]
    ppermute x1, starting transfers between devices: 1.92 us -> 3.28 us  [on_device(): other_pair = lax.ppermute(pair, 'grp', partners(1))]
where the time goes in v11:
time: 86.5 us; the launch traced here: 86.3 us
  blocking collectives  55.2 us (64%)
  waiting for transfers between devices  15.1 us (17%)
  starting transfers between devices  13 us (15%)
  Pallas kernels  2.95 us (3%)
    all_to_all x2, blocking collectives, exchange(): lax.all_to_all(value, 'grp', 0, 0, tiled=True, axis_index_groups=PLANES)  55.2 us
    ppermute x1, starting transfers between devices, on_device(): pair = partial + lax.ppermute(partial, 'grp', partners(0))  9.69 us
    ppermute x1, waiting for transfers between devices, on_device(): pair = partial + lax.ppermute(partial, 'grp', partners(0))  7.75 us
    ppermute x1, waiting for transfers between devices, on_device(): other_pair = lax.ppermute(pair, 'grp', partners(1))  7.38 us
    ppermute x1, starting transfers between devices, on_device(): other_pair = lax.ppermute(pair, 'grp', partners(1))  3.28 us
  transfers between devices with their start and end apart: 2, of which 2 were waited for; matrix products, arithmetic and copies ran while one was open for 0% of the time, Pallas kernels for 0%

profile of v11, /device:TPU:1, one launch (start us, length us, event | category | flops | bytes accessed | tf_op | source)
XLA Modules:
  0.0 86.3 jit_solution(1903746280205003834)
XLA Ops:
  0.0 1.3 %shard_map.37 = f32[1040,128]{1,0:T(8,128)S(1)} custom-call(s32[2,8]{1,0:T(2,128)} %table_hbm.1, s32[2]{0:T(128)} %coefs_hbm.1, f32[16,64,128]{2,1,0:T(8,128)} %bitcast.8), custom_call_target="tpu_custom_call" | custom-call | tf_op jit(solution)/shard_map/pallas_call | solution.py:161
  1.3 30.8 %all_to_all.10 = f32[16,1,8320]{2,1,0:T(1,128)S(1)} all-to-all(f32[16,1,8320]{2,1,0:T(1,128)S(1)} %bitcast.6), channel_id=1, replica_groups={{0,12,96,108,192,204,288,300,384,396,480,492,576,588,672,684},{24,36,12..., dimensions={0} | all-to-all | bytes 1064960 | tf_op jit(solution)/shard_map/all_to_all | solution.py:37
  32.1 0.3 shard_map.38
  32.4 9.7 %collective-permute-start = (f32[4,64,128]{2,1,0:T(8,128)S(1)}, f32[4,64,128]{2,1,0:T(8,128)S(1)}, u32[]{:S(2)}, u32[]{:S(2)}) collective-permute-start(f32[4,64,128]{2,1,0:T(8,128)S(1)} %get-tuple-element.7), channel_id=1, source_target_pairs={{0,72},{12,84},{24,48},{36,60},{48,24},{60,36},{72,0},{84,12},{96,... | collective-permute-start | bytes 393224 | tf_op jit(solution)/shard_map/ppermute | solution.py:186
  42.1 7.7 %collective-permute-done = f32[4,64,128]{2,1,0:T(8,128)S(1)} collective-permute-done((f32[4,64,128]{2,1,0:T(8,128)S(1)}, f32[4,64,128]{2,1,0:T(8,128)S(1)}, u32[]{:S(2)}, u32[]{:S(2)}) %collective-permute-start) | collective-permute-done | bytes 131104 | tf_op jit(solution)/shard_map/ppermute | solution.py:186
  49.9 3.3 %collective-permute-start.1 = (f32[4,64,128]{2,1,0:T(8,128)S(1)}, f32[4,64,128]{2,1,0:T(8,128)S(1)}, u32[]{:S(2)}, u32[]{:S(2)}) collective-permute-start(f32[4,64,128]{2,1,0:T(8,128)S(1)} %add.3.pair_ref), channel_id=1, source_target_pairs={{0,24},{12,36},{24,0},{36,12},{48,72},{60,84},{72,48},{84,60},{96,... | collective-permute-start | bytes 393224 | tf_op jit(solution)/shard_map/ppermute | solution.py:187
  53.2 7.4 %collective-permute-done.1.other_pair_ref = f32[4,64,128]{2,1,0:T(8,128)S(1)} collective-permute-done((f32[4,64,128]{2,1,0:T(8,128)S(1)}, f32[4,64,128]{2,1,0:T(8,128)S(1)}, u32[]{:S(2)}, u32[]{:S(2)}) %collective-permute-start.1) | collective-permute-done | bytes 131104 | tf_op jit(solution)/shard_map/ppermute | solution.py:187
  60.5 0.4 shard_map.39
  61.0 24.3 %all_to_all.11 = f32[16,64,128]{2,1,0:T(8,128)S(1)} all-to-all(f32[16,64,128]{2,1,0:T(8,128)S(1)} %shard_map.39), channel_id=1, replica_groups={{0,12,96,108,192,204,288,300,384,396,480,492,576,588,672,684},{24,36,12..., dimensions={0} | all-to-all | bytes 1048576 | tf_op jit(solution)/shard_map/all_to_all | solution.py:37
  85.3 1.0 %shard_map.40 = f32[16,64,128]{2,1,0:T(8,128)} custom-call(f32[64,16,128]{2,1,0:T(8,128)S(1)} %bitcast.7), custom_call_target="tpu_custom_call" | custom-call | tf_op jit(solution)/shard_map/pallas_call | solution.py:196
  (1 shorter events, 0.0 us)
Async XLA Ops:
  32.4 17.4 %collective-permute-start = (f32[4,64,128]{2,1,0:T(8,128)S(1)}, f32[4,64,128]{2,1,0:T(8,128)S(1)}, u32[]{:S(2)}, u32[]{:S(2)}) collective-permute-start(f32[4,64,128]{2,1,0:T(8,128)S(1)} %get-tuple-element.7), channel_id=1, source_target_pairs={{0,72},{12,84},{24,48},{36,60},{48,24},{60,36},{72,0},{84,12},{96,... | collective-permute-start | bytes 393224 | tf_op jit(solution)/shard_map/ppermute | solution.py:186
  49.9 10.7 %collective-permute-start.1 = (f32[4,64,128]{2,1,0:T(8,128)S(1)}, f32[4,64,128]{2,1,0:T(8,128)S(1)}, u32[]{:S(2)}, u32[]{:S(2)}) collective-permute-start(f32[4,64,128]{2,1,0:T(8,128)S(1)} %add.3.pair_ref), channel_id=1, source_target_pairs={{0,24},{12,36},{24,0},{36,12},{48,72},{60,84},{72,48},{84,60},{96,... | collective-permute-start | bytes 393224 | tf_op jit(solution)/shard_map/ppermute | solution.py:187

commit v12 on v11

--- a/solution.py
+++ b/solution.py
@@ -14,7 +14,7 @@
     pairs = []
     for i in range(Y * Z * CORES):
         y, z, c = i // (Z * CORES), i // CORES % Z, i % CORES
-        other = (Z - 1 - z, z ^ 1)[turn]
+        other = z ^ 1 if turn != c else Z - 1 - z
         pairs.append((i, (y * Z + other) * CORES + c))
     return pairs
 

time: 86.5 us -> 80.9 us (0.935)
  the two profiles are of different devices: /device:TPU:1 before, /device:TPU:69 now
where the time goes in v12:
time: 80.9 us; the launch traced here: 80.7 us
  blocking collectives  49.6 us (61%)
  starting transfers between devices  22 us (27%)
  waiting for transfers between devices  6.05 us (7%)
  Pallas kernels  2.95 us (4%)
    all_to_all x2, blocking collectives, exchange(): lax.all_to_all(value, 'grp', 0, 0, tiled=True, axis_index_groups=PLANES)  49.6 us
    ppermute x1, starting transfers between devices, on_device(): other_pair = lax.ppermute(pair, 'grp', partners(1))  13.2 us
    ppermute x1, starting transfers between devices, on_device(): pair = partial + lax.ppermute(partial, 'grp', partners(0))  8.83 us
    ppermute x1, waiting for transfers between devices, on_device(): other_pair = lax.ppermute(pair, 'grp', partners(1))  3.71 us
    ppermute x1, waiting for transfers between devices, on_device(): pair = partial + lax.ppermute(partial, 'grp', partners(0))  2.34 us
  transfers between devices with their start and end apart: 2, of which 2 were waited for; matrix products, arithmetic and copies ran while one was open for 0% of the time, Pallas kernels for 0%

profile of v12, /device:TPU:69, one launch (start us, length us, event | category | flops | bytes accessed | tf_op | source)
XLA Modules:
  0.0 80.7 jit_solution(12282831291070870643)
XLA Ops:
  0.0 1.3 %shard_map.37 = f32[1040,128]{1,0:T(8,128)S(1)} custom-call(s32[2,8]{1,0:T(2,128)} %table_hbm.1, s32[2]{0:T(128)} %coefs_hbm.1, f32[16,64,128]{2,1,0:T(8,128)} %bitcast.8), custom_call_target="tpu_custom_call" | custom-call | tf_op jit(solution)/shard_map/pallas_call | solution.py:161
  1.3 25.4 %all_to_all.10 = f32[16,1,8320]{2,1,0:T(1,128)S(1)} all-to-all(f32[16,1,8320]{2,1,0:T(1,128)S(1)} %bitcast.6), channel_id=1, replica_groups={{0,12,96,108,192,204,288,300,384,396,480,492,576,588,672,684},{24,36,12..., dimensions={0} | all-to-all | bytes 1064960 | tf_op jit(solution)/shard_map/all_to_all | solution.py:37
  26.7 0.3 shard_map.38
  27.0 8.8 %collective-permute-start = (f32[4,64,128]{2,1,0:T(8,128)S(1)}, f32[4,64,128]{2,1,0:T(8,128)S(1)}, u32[]{:S(2)}, u32[]{:S(2)}) collective-permute-start(f32[4,64,128]{2,1,0:T(8,128)S(1)} %get-tuple-element.7), channel_id=1, source_target_pairs={{0,72},{12,36},{24,48},{36,12},{48,24},{60,84},{72,0},{84,60},{96,... | collective-permute-start | bytes 393224 | tf_op jit(solution)/shard_map/ppermute | solution.py:186
  35.8 2.3 %collective-permute-done = f32[4,64,128]{2,1,0:T(8,128)S(1)} collective-permute-done((f32[4,64,128]{2,1,0:T(8,128)S(1)}, f32[4,64,128]{2,1,0:T(8,128)S(1)}, u32[]{:S(2)}, u32[]{:S(2)}) %collective-permute-start) | collective-permute-done | bytes 131104 | tf_op jit(solution)/shard_map/ppermute | solution.py:186
  38.2 13.2 %collective-permute-start.1 = (f32[4,64,128]{2,1,0:T(8,128)S(1)}, f32[4,64,128]{2,1,0:T(8,128)S(1)}, u32[]{:S(2)}, u32[]{:S(2)}) collective-permute-start(f32[4,64,128]{2,1,0:T(8,128)S(1)} %add.3.pair_ref), channel_id=1, source_target_pairs={{0,24},{12,84},{24,0},{36,60},{48,72},{60,36},{72,48},{84,12},{96,... | collective-permute-start | bytes 393224 | tf_op jit(solution)/shard_map/ppermute | solution.py:187
  51.4 3.7 %collective-permute-done.1.other_pair_ref = f32[4,64,128]{2,1,0:T(8,128)S(1)} collective-permute-done((f32[4,64,128]{2,1,0:T(8,128)S(1)}, f32[4,64,128]{2,1,0:T(8,128)S(1)}, u32[]{:S(2)}, u32[]{:S(2)}) %collective-permute-start.1) | collective-permute-done | bytes 131104 | tf_op jit(solution)/shard_map/ppermute | solution.py:187
  55.1 0.4 shard_map.39
  55.5 24.2 %all_to_all.11 = f32[16,64,128]{2,1,0:T(8,128)S(1)} all-to-all(f32[16,64,128]{2,1,0:T(8,128)S(1)} %shard_map.39), channel_id=1, replica_groups={{0,12,96,108,192,204,288,300,384,396,480,492,576,588,672,684},{24,36,12..., dimensions={0} | all-to-all | bytes 1048576 | tf_op jit(solution)/shard_map/all_to_all | solution.py:37
  79.7 1.0 %shard_map.40 = f32[16,64,128]{2,1,0:T(8,128)} custom-call(f32[64,16,128]{2,1,0:T(8,128)S(1)} %bitcast.7), custom_call_target="tpu_custom_call" | custom-call | tf_op jit(solution)/shard_map/pallas_call | solution.py:196
  (1 shorter events, 0.0 us)
Async XLA Ops:
  27.0 11.2 %collective-permute-start = (f32[4,64,128]{2,1,0:T(8,128)S(1)}, f32[4,64,128]{2,1,0:T(8,128)S(1)}, u32[]{:S(2)}, u32[]{:S(2)}) collective-permute-start(f32[4,64,128]{2,1,0:T(8,128)S(1)} %get-tuple-element.7), channel_id=1, source_target_pairs={{0,72},{12,36},{24,48},{36,12},{48,24},{60,84},{72,0},{84,60},{96,... | collective-permute-start | bytes 393224 | tf_op jit(solution)/shard_map/ppermute | solution.py:186
  38.2 16.9 %collective-permute-start.1 = (f32[4,64,128]{2,1,0:T(8,128)S(1)}, f32[4,64,128]{2,1,0:T(8,128)S(1)}, u32[]{:S(2)}, u32[]{:S(2)}) collective-permute-start(f32[4,64,128]{2,1,0:T(8,128)S(1)} %add.3.pair_ref), channel_id=1, source_target_pairs={{0,24},{12,84},{24,0},{36,60},{48,72},{60,36},{72,48},{84,12},{96,... | collective-permute-start | bytes 393224 | tf_op jit(solution)/shard_map/ppermute | solution.py:187

commit v13 on v6

--- a/solution.py
+++ b/solution.py
@@ -8,7 +8,11 @@
 SUBS = 64
 Y, Z, CORES = 8, 4, 2
 PLANES = [[(y * Z + z) * CORES + c for y in range(Y) for c in range(CORES)] for z in range(Z)]
-COLUMNS = [[(y * Z + z) * CORES + c for z in range(Z)] for y in range(Y) for c in range(CORES)]
+COLUMNS = [
+    [(y * Z + (Z - 1 - z if c else z)) * CORES + c for z in range(Z)]
+    for y in range(Y)
+    for c in range(CORES)
+]
 PEERS = Y * CORES
 COUNT = 16
 FIELDS = 64

time: 79.9 us -> 80.4 us (level)
  no operation moved by 1% of the time
where the time goes in v13:
time: 80.4 us; the launch traced here: 80.2 us
  blocking collectives  77.2 us (96%)
  Pallas kernels  2.94 us (4%)
    all_to_all x2, blocking collectives, exchange(): lax.all_to_all(value, 'grp', 0, 0, tiled=True, axis_index_groups=PLANES)  53 us
    all_gather x1, blocking collectives, on_device(): every = lax.all_gather(partial, 'grp', axis_index_groups=COLUMNS)  24.2 us

profile of v13, /device:TPU:1, one launch (start us, length us, event | category | flops | bytes accessed | tf_op | source)
XLA Modules:
  0.0 80.2 jit_solution(8194456563594570055)
XLA Ops:
  0.0 1.3 %shard_map.37 = f32[1040,128]{1,0:T(8,128)S(1)} custom-call(s32[2,8]{1,0:T(2,128)} %table_hbm.1, s32[2]{0:T(128)} %coefs_hbm.1, f32[16,64,128]{2,1,0:T(8,128)} %bitcast.10), custom_call_target="tpu_custom_call" | custom-call | tf_op jit(solution)/shard_map/pallas_call | solution.py:161
  1.3 30.8 %all_to_all.10 = f32[16,1,8320]{2,1,0:T(1,128)S(1)} all-to-all(f32[16,1,8320]{2,1,0:T(1,128)S(1)} %bitcast.7), channel_id=1, replica_groups={{0,12,96,108,192,204,288,300,384,396,480,492,576,588,672,684},{24,36,12..., dimensions={0} | all-to-all | bytes 1064960 | tf_op jit(solution)/shard_map/all_to_all | solution.py:31
  32.1 0.3 shard_map.38
  32.4 24.2 %all-gather = f32[16,64,128]{2,1,0:T(8,128)S(1)} all-gather(f32[4,64,128]{2,1,0:T(8,128)S(1)} %get-tuple-element.7), channel_id=2, replica_groups={{0,24,48,72},{84,60,36,12},{96,120,144,168},{180,156,132,108},{192,216,..., dimensions={0}, use_global_device_ids=true | all-gather | bytes 655360 | tf_op jit(solution)/shard_map/all_gather | solution.py:186
  56.6 0.4 shard_map.39
  57.0 22.2 %all_to_all.11 = f32[16,64,128]{2,1,0:T(8,128)S(1)} all-to-all(f32[16,64,128]{2,1,0:T(8,128)S(1)} %shard_map.39), channel_id=1, replica_groups={{0,12,96,108,192,204,288,300,384,396,480,492,576,588,672,684},{24,36,12..., dimensions={0} | all-to-all | bytes 1048576 | tf_op jit(solution)/shard_map/all_to_all | solution.py:31
  79.2 1.0 %shard_map.40 = f32[16,64,128]{2,1,0:T(8,128)} custom-call(f32[64,16,128]{2,1,0:T(8,128)S(1)} %bitcast.9), custom_call_target="tpu_custom_call" | custom-call | tf_op jit(solution)/shard_map/pallas_call | solution.py:195

commit v14 on v12

--- a/solution.py
+++ b/solution.py
@@ -10,12 +10,17 @@
 PLANES = [[(y * Z + z) * CORES + c for y in range(Y) for c in range(CORES)] for z in range(Z)]
 
 
+X, Z_LOW = 4, 3
+
+
 def partners(turn):
     pairs = []
     for i in range(Y * Z * CORES):
         y, z, c = i // (Z * CORES), i // CORES % Z, i % CORES
-        other = z ^ 1 if turn != c else Z - 1 - z
-        pairs.append((i, (y * Z + other) * CORES + c))
+        for dom in range(X * Z_LOW):
+            first = c if dom % Z_LOW else 1 - c
+            other = z ^ 1 if turn == first else Z - 1 - z
+            pairs.append((i * X * Z_LOW + dom, ((y * Z + other) * CORES + c) * X * Z_LOW + dom))
     return pairs
 
 
@@ -28,6 +33,7 @@
 MESSAGE = ROWS + 1
 TILE = 8
 CHUNKS = 4
+HALVES = 2
 VMEM = pl.BlockSpec(memory_space=pltpu.VMEM)
 ROOM = pltpu.CompilerParams(vmem_limit_bytes=8 << 20)
 HBM = pl.BlockSpec(memory_space=pltpu.HBM)
@@ -143,14 +149,25 @@
 
 
 def unpack_kernel(back_ref, out_hbm, held, sem):
-    chunk = COUNT // CHUNKS
-    copies = []
-    for i in range(CHUNKS):
+    direct = COUNT // 2
+    chunk = (COUNT - direct) // HALVES
+    copies = [
+        pltpu.make_async_copy(back_ref.at[:, r, :], out_hbm.at[r], sem.at[r])
+        for r in range(direct)
+    ]
+    for copy in copies:
+        copy.start()
+    for i in range(HALVES):
         for r in range(i * chunk, (i + 1) * chunk):
             for f in range(0, FIELDS, TILE):
-                held[r, f : f + TILE, :] = back_ref[f : f + TILE, r, :]
-        span = pl.ds(i * chunk, chunk)
-        copies.append(pltpu.make_async_copy(held.at[span], out_hbm.at[span], sem.at[i]))
+                held[r, f : f + TILE, :] = back_ref[f : f + TILE, direct + r, :]
+        copies.append(
+            pltpu.make_async_copy(
+                held.at[pl.ds(i * chunk, chunk)],
+                out_hbm.at[pl.ds(direct + i * chunk, chunk)],
+                sem.at[direct + i],
+            )
+        )
         copies[-1].start()
     for copy in copies:
         copy.wait()
@@ -183,8 +200,8 @@
         out_specs=(VMEM, VMEM),
         compiler_params=ROOM,
     )(got.reshape(PEERS * MESSAGE, POINTS))
-    pair = partial + lax.ppermute(partial, "grp", partners(0))
-    other_pair = lax.ppermute(pair, "grp", partners(1))
+    pair = partial + lax.ppermute(partial, ("grp", "dom"), partners(0))
+    other_pair = lax.ppermute(pair, ("grp", "dom"), partners(1))
     picks = pl.pallas_call(
         pick_kernel,
         out_shape=jax.ShapeDtypeStruct((PEERS, ROWS, POINTS), f32),
@@ -199,8 +216,8 @@
         in_specs=[VMEM],
         out_specs=HBM,
         scratch_shapes=[
-            pltpu.VMEM((COUNT, FIELDS, POINTS), f32),
-            pltpu.SemaphoreType.DMA((CHUNKS,)),
+            pltpu.VMEM((COUNT // 2, FIELDS, POINTS), f32),
+            pltpu.SemaphoreType.DMA((COUNT // 2 + HALVES,)),
         ],
         compiler_params=ROOM,
     )(back)

time: 80.9 us -> 81 us (level)
  the two profiles are of different devices: /device:TPU:69 before, /device:TPU:1 now
where the time goes in v14:
time: 81 us; the launch traced here: 80.7 us
  blocking collectives  52.5 us (65%)
  starting transfers between devices  17 us (21%)
  waiting for transfers between devices  8.33 us (10%)
  Pallas kernels  2.87 us (4%)
    all_to_all x2, blocking collectives, exchange(): lax.all_to_all(value, 'grp', 0, 0, tiled=True, axis_index_groups=PLANES)  52.5 us
    ppermute x1, starting transfers between devices, on_device(): other_pair = lax.ppermute(pair, ('grp', 'dom'), partners(1))  14 us
    ppermute x1, waiting for transfers between devices, on_device(): pair = partial + lax.ppermute(partial, ('grp', 'dom'), partners(0))  4.48 us
    ppermute x1, waiting for transfers between devices, on_device(): other_pair = lax.ppermute(pair, ('grp', 'dom'), partners(1))  3.85 us
    ppermute x1, starting transfers between devices, on_device(): pair = partial + lax.ppermute(partial, ('grp', 'dom'), partners(0))  3.02 us
  transfers between devices with their start and end apart: 2, of which 2 were waited for; matrix products, arithmetic and copies ran while one was open for 0% of the time, Pallas kernels for 0%

profile of v14, /device:TPU:1, one launch (start us, length us, event | category | flops | bytes accessed | tf_op | source)
XLA Modules:
  0.0 80.7 jit_solution(10872049248665911798)
XLA Ops:
  0.0 1.3 %shard_map.37 = f32[1040,128]{1,0:T(8,128)S(1)} custom-call(s32[2,8]{1,0:T(2,128)} %table_hbm.1, s32[2]{0:T(128)} %coefs_hbm.1, f32[16,64,128]{2,1,0:T(8,128)} %bitcast.8), custom_call_target="tpu_custom_call" | custom-call | tf_op jit(solution)/shard_map/pallas_call | solution.py:178
  1.3 30.8 %all_to_all.10 = f32[16,1,8320]{2,1,0:T(1,128)S(1)} all-to-all(f32[16,1,8320]{2,1,0:T(1,128)S(1)} %bitcast.6), channel_id=1, replica_groups={{0,12,96,108,192,204,288,300,384,396,480,492,576,588,672,684},{24,36,12..., dimensions={0} | all-to-all | bytes 1064960 | tf_op jit(solution)/shard_map/all_to_all | solution.py:43
  32.1 0.3 shard_map.38
  32.4 3.0 %collective-permute-start = (f32[4,64,128]{2,1,0:T(8,128)S(1)}, f32[4,64,128]{2,1,0:T(8,128)S(1)}, u32[]{:S(2)}, u32[]{:S(2)}) collective-permute-start(f32[4,64,128]{2,1,0:T(8,128)S(1)} %get-tuple-element.7), channel_id=1, source_target_pairs={{0,72},{1,25},{2,26},{3,75},{4,28},{5,29},{6,78},{7,31},{8,32},{9,... | collective-permute-start | bytes 393224 | tf_op jit(solution)/shard_map/ppermute | solution.py:203
  35.4 4.5 %collective-permute-done = f32[4,64,128]{2,1,0:T(8,128)S(1)} collective-permute-done((f32[4,64,128]{2,1,0:T(8,128)S(1)}, f32[4,64,128]{2,1,0:T(8,128)S(1)}, u32[]{:S(2)}, u32[]{:S(2)}) %collective-permute-start) | collective-permute-done | bytes 131104 | tf_op jit(solution)/shard_map/ppermute | solution.py:203
  39.9 14.0 %collective-permute-start.1 = (f32[4,64,128]{2,1,0:T(8,128)S(1)}, f32[4,64,128]{2,1,0:T(8,128)S(1)}, u32[]{:S(2)}, u32[]{:S(2)}) collective-permute-start(f32[4,64,128]{2,1,0:T(8,128)S(1)} %add.3.pair_ref), channel_id=1, source_target_pairs={{0,24},{1,73},{2,74},{3,27},{4,76},{5,77},{6,30},{7,79},{8,80},{9,... | collective-permute-start | bytes 393224 | tf_op jit(solution)/shard_map/ppermute | solution.py:204
  54.0 3.8 %collective-permute-done.1.other_pair_ref = f32[4,64,128]{2,1,0:T(8,128)S(1)} collective-permute-done((f32[4,64,128]{2,1,0:T(8,128)S(1)}, f32[4,64,128]{2,1,0:T(8,128)S(1)}, u32[]{:S(2)}, u32[]{:S(2)}) %collective-permute-start.1) | collective-permute-done | bytes 131104 | tf_op jit(solution)/shard_map/ppermute | solution.py:204
  57.8 0.4 shard_map.39
  58.2 21.6 %all_to_all.11 = f32[16,64,128]{2,1,0:T(8,128)S(1)} all-to-all(f32[16,64,128]{2,1,0:T(8,128)S(1)} %shard_map.39), channel_id=1, replica_groups={{0,12,96,108,192,204,288,300,384,396,480,492,576,588,672,684},{24,36,12..., dimensions={0} | all-to-all | bytes 1048576 | tf_op jit(solution)/shard_map/all_to_all | solution.py:43
  79.8 0.9 %shard_map.40 = f32[16,64,128]{2,1,0:T(8,128)} custom-call(f32[64,16,128]{2,1,0:T(8,128)S(1)} %bitcast.7), custom_call_target="tpu_custom_call" | custom-call | tf_op jit(solution)/shard_map/pallas_call | solution.py:213
  (1 shorter events, 0.0 us)
Async XLA Ops:
  32.4 7.5 %collective-permute-start = (f32[4,64,128]{2,1,0:T(8,128)S(1)}, f32[4,64,128]{2,1,0:T(8,128)S(1)}, u32[]{:S(2)}, u32[]{:S(2)}) collective-permute-start(f32[4,64,128]{2,1,0:T(8,128)S(1)} %get-tuple-element.7), channel_id=1, source_target_pairs={{0,72},{1,25},{2,26},{3,75},{4,28},{5,29},{6,78},{7,31},{8,32},{9,... | collective-permute-start | bytes 393224 | tf_op jit(solution)/shard_map/ppermute | solution.py:203
  39.9 17.9 %collective-permute-start.1 = (f32[4,64,128]{2,1,0:T(8,128)S(1)}, f32[4,64,128]{2,1,0:T(8,128)S(1)}, u32[]{:S(2)}, u32[]{:S(2)}) collective-permute-start(f32[4,64,128]{2,1,0:T(8,128)S(1)} %add.3.pair_ref), channel_id=1, source_target_pairs={{0,24},{1,73},{2,74},{3,27},{4,76},{5,77},{6,30},{7,79},{8,80},{9,... | collective-permute-start | bytes 393224 | tf_op jit(solution)/shard_map/ppermute | solution.py:204

commit v15 on v6

--- a/solution.py
+++ b/solution.py
@@ -3,12 +3,11 @@
 from jax import lax
 from jax.experimental import pallas as pl
 from jax.experimental.pallas import tpu as pltpu
+from jax.sharding import Mesh
 from jax.sharding import PartitionSpec as P
 
 SUBS = 64
 Y, Z, CORES = 8, 4, 2
-PLANES = [[(y * Z + z) * CORES + c for y in range(Y) for c in range(CORES)] for z in range(Z)]
-COLUMNS = [[(y * Z + z) * CORES + c for z in range(Z)] for y in range(Y) for c in range(CORES)]
 PEERS = Y * CORES
 COUNT = 16
 FIELDS = 64
@@ -24,7 +23,7 @@
 
 
 def exchange(value):
-    return lax.all_to_all(value, "grp", 0, 0, tiled=True, axis_index_groups=PLANES)
+    return lax.all_to_all(value, ("y", "core"), 0, 0, tiled=True)
 
 
 def in_hbm(value):
@@ -179,7 +178,7 @@
         out_specs=(VMEM, VMEM),
         compiler_params=ROOM,
     )(got.reshape(PEERS * MESSAGE, POINTS))
-    every = lax.all_gather(partial, "grp", axis_index_groups=COLUMNS)
+    every = lax.all_gather(partial, "z")
     picks = pl.pallas_call(
         pick_kernel,
         out_shape=jax.ShapeDtypeStruct((PEERS, ROWS, POINTS), f32),
@@ -203,10 +202,12 @@
 
 
 def solution(mesh):
+    parts = Mesh(mesh.devices.reshape(Y, Z, CORES, -1), ("y", "z", "core", "dom"))
+    grp = ("y", "z", "core")
     return jax.shard_map(
         on_device,
-        mesh=mesh,
-        in_specs=(P("grp", None, None, "dom"), P("grp", None), P("grp")),
-        out_specs=P("grp", None, None, "dom"),
+        mesh=parts,
+        in_specs=(P(grp, None, None, "dom"), P(grp, None), P(grp)),
+        out_specs=P(grp, None, None, "dom"),
         check_vma=False,
     )

time: 79.9 us -> 79.9 us (level)
  no operation moved by 1% of the time
where the time goes in v15:
time: 79.9 us; the launch traced here: 79.7 us
  blocking collectives  76.7 us (96%)
  Pallas kernels  2.94 us (4%)
    all_to_all x2, blocking collectives, exchange(): return lax.all_to_all(value, ('y', 'core'), 0, 0, tiled=True)  52.5 us
    all_gather x1, blocking collectives, on_device(): every = lax.all_gather(partial, 'z')  24.2 us

profile of v15, /device:TPU:1, one launch (start us, length us, event | category | flops | bytes accessed | tf_op | source)
XLA Modules:
  0.0 79.7 jit_solution(1000580298963826748)
XLA Ops:
  0.0 1.3 %shard_map.37 = f32[1040,128]{1,0:T(8,128)S(1)} custom-call(s32[2,8]{1,0:T(2,128)} %table_hbm.1, s32[2]{0:T(128)} %coefs_hbm.1, f32[16,64,128]{2,1,0:T(8,128)} %bitcast.10), custom_call_target="tpu_custom_call" | custom-call | tf_op jit(solution)/shard_map/pallas_call | solution.py:156
  1.3 30.8 %all_to_all.10 = f32[16,1,8320]{2,1,0:T(1,128)S(1)} all-to-all(f32[16,1,8320]{2,1,0:T(1,128)S(1)} %bitcast.7), channel_id=1, replica_groups=mesh['y'=8,'z'=4,'core'=2,'dom'=12] {'y','core'}, dimensions={0} | all-to-all | bytes 1064960 | tf_op jit(solution)/shard_map/all_to_all | solution.py:26
  32.1 0.3 shard_map.38
  32.4 24.2 %all-gather = f32[16,64,128]{2,1,0:T(8,128)S(1)} all-gather(f32[4,64,128]{2,1,0:T(8,128)S(1)} %get-tuple-element.7), channel_id=2, replica_groups=mesh['y'=8,'z'=4,'core'=2,'dom'=12] {'z'}, dimensions={0}, use_global_device_ids=true | all-gather | bytes 655360 | tf_op jit(solution)/shard_map/all_gather | solution.py:181
  56.6 0.4 shard_map.39
  57.0 21.7 %all_to_all.11 = f32[16,64,128]{2,1,0:T(8,128)S(1)} all-to-all(f32[16,64,128]{2,1,0:T(8,128)S(1)} %shard_map.39), channel_id=1, replica_groups=mesh['y'=8,'z'=4,'core'=2,'dom'=12] {'y','core'}, dimensions={0} | all-to-all | bytes 1048576 | tf_op jit(solution)/shard_map/all_to_all | solution.py:26
  78.7 1.0 %shard_map.40 = f32[16,64,128]{2,1,0:T(8,128)} custom-call(f32[64,16,128]{2,1,0:T(8,128)S(1)} %bitcast.9), custom_call_target="tpu_custom_call" | custom-call | tf_op jit(solution)/shard_map/pallas_call | solution.py:190

commit v16 on v9

--- a/solution.py
+++ b/solution.py
@@ -10,9 +10,14 @@
 PLANES = [[(y * Z + z) * CORES + c for y in range(Y) for c in range(CORES)] for z in range(Z)]
 
 
-def along_z(step):
-    places = [(y, z, c) for y in range(Y) for z in range(Z) for c in range(CORES)]
-    return [(i, (y * Z + (z + step) % Z) * CORES + c) for i, (y, z, c) in enumerate(places)]
+def couples(turn):
+    near, wrapped = [(0, 1), (2, 3)], [(1, 2), (0, 3)]
+    return [
+        [(y * Z + z) * CORES + c for z in couple]
+        for y in range(Y)
+        for c in range(CORES)
+        for couple in (near if turn == c else wrapped)
+    ]
 
 
 PEERS = Y * CORES
@@ -123,10 +128,8 @@
     labels_ref[...] = jnp.broadcast_to(labels, labels_ref.shape)
 
 
-def pick_kernel(own_ref, far_ref, below_ref, above_ref, labels_ref, out_ref):
-    sparse = jnp.concatenate(
-        [(own_ref[j] + far_ref[j]) + (below_ref[j] + above_ref[j]) for j in range(OWN)], axis=1
-    )
+def pick_kernel(pairs_ref, labels_ref, out_ref):
+    sparse = jnp.concatenate([pairs_ref[0, j] + pairs_ref[1, j] for j in range(OWN)], axis=1)
     wanted = lax.broadcasted_iota(jnp.int32, (SUBS, PEERS * COUNT), 0).astype(jnp.float32)
     onehot = (labels_ref[0:1, :] == wanted).astype(jnp.float32).T.astype(jnp.bfloat16)
     picks = jnp.dot(
@@ -181,14 +184,15 @@
         out_specs=(VMEM, VMEM),
         compiler_params=ROOM,
     )(got.reshape(PEERS * MESSAGE, POINTS))
-    others = [lax.ppermute(partial, "grp", along_z(step)) for step in (2, 1, 3)]
+    pair = jnp.sum(lax.all_gather(partial, "grp", axis_index_groups=couples(0)), axis=0)
+    pairs = lax.all_gather(pair, "grp", axis_index_groups=couples(1))
     picks = pl.pallas_call(
         pick_kernel,
         out_shape=jax.ShapeDtypeStruct((PEERS, ROWS, POINTS), f32),
-        in_specs=[VMEM] * 5,
+        in_specs=[VMEM, VMEM],
         out_specs=VMEM,
         compiler_params=ROOM,
-    )(partial, *others, labels)
+    )(pairs, labels)
     back = exchange(picks).reshape(FIELDS, COUNT, POINTS)
     combined = pl.pallas_call(
         unpack_kernel,

time: 85.8 us -> 77.5 us (0.903)
  the two profiles are of different devices: /device:TPU:131 before, /device:TPU:1 now
where the time goes in v16:
time: 77.5 us; the launch traced here: 77.3 us
  blocking collectives  74.3 us (96%)
  Pallas kernels  2.94 us (4%)
    all_to_all x2, blocking collectives, exchange(): lax.all_to_all(value, 'grp', 0, 0, tiled=True, axis_index_groups=PLANES)  53.9 us
    all_gather x1, blocking collectives, on_device(): lax.all_gather(partial, 'grp', axis_index_groups=couples(0))  13.2 us
    all_gather x1, blocking collectives, on_device(): pairs = lax.all_gather(pair, 'grp', axis_index_groups=couples(1))  7.15 us

profile of v16, /device:TPU:1, one launch (start us, length us, event | category | flops | bytes accessed | tf_op | source)
XLA Modules:
  0.0 77.3 jit_solution(7585196878379879758)
XLA Ops:
  0.0 1.3 %shard_map.37 = f32[1040,128]{1,0:T(8,128)S(1)} custom-call(s32[2,8]{1,0:T(2,128)} %table_hbm.1, s32[2]{0:T(128)} %coefs_hbm.1, f32[16,64,128]{2,1,0:T(8,128)} %bitcast.12), custom_call_target="tpu_custom_call" | custom-call | tf_op jit(solution)/shard_map/pallas_call | solution.py:162
  1.3 30.8 %all_to_all.10 = f32[16,1,8320]{2,1,0:T(1,128)S(1)} all-to-all(f32[16,1,8320]{2,1,0:T(1,128)S(1)} %bitcast.8), channel_id=1, replica_groups={{0,12,96,108,192,204,288,300,384,396,480,492,576,588,672,684},{24,36,12..., dimensions={0} | all-to-all | bytes 1064960 | tf_op jit(solution)/shard_map/all_to_all | solution.py:38
  32.1 0.3 shard_map.38
  32.4 13.2 %all-gather = f32[8,64,128]{2,1,0:T(8,128)S(1)} all-gather(f32[4,64,128]{2,1,0:T(8,128)S(1)} %get-tuple-element.7), channel_id=2, replica_groups={{0,24},{48,72},{36,60},{12,84},{96,120},{144,168},{132,156},{108,180},{..., dimensions={0}, use_global_device_ids=true | all-gather | bytes 393216 | tf_op jit(solution)/shard_map/all_gather | solution.py:187
  45.6 7.1 %all-gather.1 = f32[8,64,128]{2,1,0:T(8,128)S(1)} all-gather(f32[4,64,128]{2,1,0:T(8,128)S(1)} %reduce_sum.9), channel_id=3, replica_groups={{24,48},{0,72},{12,36},{60,84},{120,144},{96,168},{108,132},{156,180},{..., dimensions={0}, use_global_device_ids=true | all-gather | bytes 393216 | tf_op jit(solution)/shard_map/all_gather | solution.py:188
  52.8 0.4 shard_map.39
  53.2 23.1 %all_to_all.11 = f32[16,64,128]{2,1,0:T(8,128)S(1)} all-to-all(f32[16,64,128]{2,1,0:T(8,128)S(1)} %shard_map.39), channel_id=1, replica_groups={{0,12,96,108,192,204,288,300,384,396,480,492,576,588,672,684},{24,36,12..., dimensions={0} | all-to-all | bytes 1048576 | tf_op jit(solution)/shard_map/all_to_all | solution.py:38
  76.3 1.0 %shard_map.40 = f32[16,64,128]{2,1,0:T(8,128)} custom-call(f32[64,16,128]{2,1,0:T(8,128)S(1)} %bitcast.9), custom_call_target="tpu_custom_call" | custom-call | tf_op jit(solution)/shard_map/pallas_call | solution.py:197
  (1 shorter events, 0.0 us)

commit v17 on v16

--- a/solution.py
+++ b/solution.py
@@ -16,7 +16,7 @@
         [(y * Z + z) * CORES + c for z in couple]
         for y in range(Y)
         for c in range(CORES)
-        for couple in (near if turn == c else wrapped)
+        for couple in (wrapped if turn == c else near)
     ]
 
 
@@ -29,6 +29,7 @@
 MESSAGE = ROWS + 1
 TILE = 8
 CHUNKS = 4
+HALVES = 2
 VMEM = pl.BlockSpec(memory_space=pltpu.VMEM)
 ROOM = pltpu.CompilerParams(vmem_limit_bytes=8 << 20)
 HBM = pl.BlockSpec(memory_space=pltpu.HBM)
@@ -144,14 +145,25 @@
 
 
 def unpack_kernel(back_ref, out_hbm, held, sem):
-    chunk = COUNT // CHUNKS
-    copies = []
-    for i in range(CHUNKS):
+    direct = COUNT // 2
+    chunk = (COUNT - direct) // HALVES
+    copies = [
+        pltpu.make_async_copy(back_ref.at[:, r, :], out_hbm.at[r], sem.at[r])
+        for r in range(direct)
+    ]
+    for copy in copies:
+        copy.start()
+    for i in range(HALVES):
         for r in range(i * chunk, (i + 1) * chunk):
             for f in range(0, FIELDS, TILE):
-                held[r, f : f + TILE, :] = back_ref[f : f + TILE, r, :]
-        span = pl.ds(i * chunk, chunk)
-        copies.append(pltpu.make_async_copy(held.at[span], out_hbm.at[span], sem.at[i]))
+                held[r, f : f + TILE, :] = back_ref[f : f + TILE, direct + r, :]
+        copies.append(
+            pltpu.make_async_copy(
+                held.at[pl.ds(i * chunk, chunk)],
+                out_hbm.at[pl.ds(direct + i * chunk, chunk)],
+                sem.at[direct + i],
+            )
+        )
         copies[-1].start()
     for copy in copies:
         copy.wait()
@@ -200,8 +212,8 @@
         in_specs=[VMEM],
         out_specs=HBM,
         scratch_shapes=[
-            pltpu.VMEM((COUNT, FIELDS, POINTS), f32),
-            pltpu.SemaphoreType.DMA((CHUNKS,)),
+            pltpu.VMEM((COUNT // 2, FIELDS, POINTS), f32),
+            pltpu.SemaphoreType.DMA((COUNT // 2 + HALVES,)),
         ],
         compiler_params=ROOM,
     )(back)

time: 77.5 us -> 78.4 us (1.012)
  the two profiles are of different devices: /device:TPU:1 before, /device:TPU:67 now
where the time goes in v17:
time: 78.4 us; the launch traced here: 78.2 us
  blocking collectives  75.3 us (96%)
  Pallas kernels  2.86 us (4%)
    all_to_all x2, blocking collectives, exchange(): lax.all_to_all(value, 'grp', 0, 0, tiled=True, axis_index_groups=PLANES)  49.6 us
    all_gather x1, blocking collectives, on_device(): pairs = lax.all_gather(pair, 'grp', axis_index_groups=couples(1))  15.7 us
    all_gather x1, blocking collectives, on_device(): lax.all_gather(partial, 'grp', axis_index_groups=couples(0))  9.93 us

profile of v17, /device:TPU:67, one launch (start us, length us, event | category | flops | bytes accessed | tf_op | source)
XLA Modules:
  0.0 78.2 jit_solution(4322788419271325601)
XLA Ops:
  0.0 1.3 %shard_map.37 = f32[1040,128]{1,0:T(8,128)S(1)} custom-call(s32[2,8]{1,0:T(2,128)} %table_hbm.1, s32[2]{0:T(128)} %coefs_hbm.1, f32[16,64,128]{2,1,0:T(8,128)} %bitcast.12), custom_call_target="tpu_custom_call" | custom-call | tf_op jit(solution)/shard_map/pallas_call | solution.py:174
  1.3 25.4 %all_to_all.10 = f32[16,1,8320]{2,1,0:T(1,128)S(1)} all-to-all(f32[16,1,8320]{2,1,0:T(1,128)S(1)} %bitcast.8), channel_id=1, replica_groups={{0,12,96,108,192,204,288,300,384,396,480,492,576,588,672,684},{24,36,12..., dimensions={0} | all-to-all | bytes 1064960 | tf_op jit(solution)/shard_map/all_to_all | solution.py:39
  26.7 0.3 shard_map.38
  27.0 9.9 %all-gather = f32[8,64,128]{2,1,0:T(8,128)S(1)} all-gather(f32[4,64,128]{2,1,0:T(8,128)S(1)} %get-tuple-element.7), channel_id=2, replica_groups={{24,48},{0,72},{12,36},{60,84},{120,144},{96,168},{108,132},{156,180},{..., dimensions={0}, use_global_device_ids=true | all-gather | bytes 393216 | tf_op jit(solution)/shard_map/all_gather | solution.py:199
  36.9 15.7 %all-gather.1 = f32[8,64,128]{2,1,0:T(8,128)S(1)} all-gather(f32[4,64,128]{2,1,0:T(8,128)S(1)} %reduce_sum.9), channel_id=3, replica_groups={{0,24},{48,72},{36,60},{12,84},{96,120},{144,168},{132,156},{108,180},{..., dimensions={0}, use_global_device_ids=true | all-gather | bytes 393216 | tf_op jit(solution)/shard_map/all_gather | solution.py:200
  52.7 0.4 shard_map.39
  53.1 24.2 %all_to_all.11 = f32[16,64,128]{2,1,0:T(8,128)S(1)} all-to-all(f32[16,64,128]{2,1,0:T(8,128)S(1)} %shard_map.39), channel_id=1, replica_groups={{0,12,96,108,192,204,288,300,384,396,480,492,576,588,672,684},{24,36,12..., dimensions={0} | all-to-all | bytes 1048576 | tf_op jit(solution)/shard_map/all_to_all | solution.py:39
  77.3 0.9 %shard_map.40 = f32[16,64,128]{2,1,0:T(8,128)} custom-call(f32[64,16,128]{2,1,0:T(8,128)S(1)} %bitcast.9), custom_call_target="tpu_custom_call" | custom-call | tf_op jit(solution)/shard_map/pallas_call | solution.py:209
  (1 shorter events, 0.0 us)

commit v18 on v17

--- a/solution.py
+++ b/solution.py
@@ -16,7 +16,7 @@
         [(y * Z + z) * CORES + c for z in couple]
         for y in range(Y)
         for c in range(CORES)
-        for couple in (wrapped if turn == c else near)
+        for couple in (near if turn == c else wrapped)
     ]
 
 

time: 78.4 us -> 77.4 us (0.987)
  the two profiles are of different devices: /device:TPU:67 before, /device:TPU:1 now
where the time goes in v18:
time: 77.4 us; the launch traced here: 77.2 us
  blocking collectives  74.3 us (96%)
  Pallas kernels  2.86 us (4%)
    all_to_all x2, blocking collectives, exchange(): lax.all_to_all(value, 'grp', 0, 0, tiled=True, axis_index_groups=PLANES)  53.9 us
    all_gather x1, blocking collectives, on_device(): lax.all_gather(partial, 'grp', axis_index_groups=couples(0))  13.2 us
    all_gather x1, blocking collectives, on_device(): pairs = lax.all_gather(pair, 'grp', axis_index_groups=couples(1))  7.15 us

profile of v18, /device:TPU:1, one launch (start us, length us, event | category | flops | bytes accessed | tf_op | source)
XLA Modules:
  0.0 77.2 jit_solution(6834568143591794393)
XLA Ops:
  0.0 1.3 %shard_map.37 = f32[1040,128]{1,0:T(8,128)S(1)} custom-call(s32[2,8]{1,0:T(2,128)} %table_hbm.1, s32[2]{0:T(128)} %coefs_hbm.1, f32[16,64,128]{2,1,0:T(8,128)} %bitcast.12), custom_call_target="tpu_custom_call" | custom-call | tf_op jit(solution)/shard_map/pallas_call | solution.py:174
  1.3 30.8 %all_to_all.10 = f32[16,1,8320]{2,1,0:T(1,128)S(1)} all-to-all(f32[16,1,8320]{2,1,0:T(1,128)S(1)} %bitcast.8), channel_id=1, replica_groups={{0,12,96,108,192,204,288,300,384,396,480,492,576,588,672,684},{24,36,12..., dimensions={0} | all-to-all | bytes 1064960 | tf_op jit(solution)/shard_map/all_to_all | solution.py:39
  32.1 0.3 shard_map.38
  32.4 13.2 %all-gather = f32[8,64,128]{2,1,0:T(8,128)S(1)} all-gather(f32[4,64,128]{2,1,0:T(8,128)S(1)} %get-tuple-element.7), channel_id=2, replica_groups={{0,24},{48,72},{36,60},{12,84},{96,120},{144,168},{132,156},{108,180},{..., dimensions={0}, use_global_device_ids=true | all-gather | bytes 393216 | tf_op jit(solution)/shard_map/all_gather | solution.py:199
  45.6 7.1 %all-gather.1 = f32[8,64,128]{2,1,0:T(8,128)S(1)} all-gather(f32[4,64,128]{2,1,0:T(8,128)S(1)} %reduce_sum.9), channel_id=3, replica_groups={{24,48},{0,72},{12,36},{60,84},{120,144},{96,168},{108,132},{156,180},{..., dimensions={0}, use_global_device_ids=true | all-gather | bytes 393216 | tf_op jit(solution)/shard_map/all_gather | solution.py:200
  52.8 0.4 shard_map.39
  53.2 23.1 %all_to_all.11 = f32[16,64,128]{2,1,0:T(8,128)S(1)} all-to-all(f32[16,64,128]{2,1,0:T(8,128)S(1)} %shard_map.39), channel_id=1, replica_groups={{0,12,96,108,192,204,288,300,384,396,480,492,576,588,672,684},{24,36,12..., dimensions={0} | all-to-all | bytes 1048576 | tf_op jit(solution)/shard_map/all_to_all | solution.py:39
  76.3 0.9 %shard_map.40 = f32[16,64,128]{2,1,0:T(8,128)} custom-call(f32[64,16,128]{2,1,0:T(8,128)S(1)} %bitcast.9), custom_call_target="tpu_custom_call" | custom-call | tf_op jit(solution)/shard_map/pallas_call | solution.py:209
  (1 shorter events, 0.0 us)

commit v19 on v16

--- a/solution.py
+++ b/solution.py
@@ -11,7 +11,7 @@
 
 
 def couples(turn):
-    near, wrapped = [(0, 1), (2, 3)], [(1, 2), (0, 3)]
+    near, wrapped = [(0, 1), (2, 3)], [(1, 2), (3, 0)]
     return [
         [(y * Z + z) * CORES + c for z in couple]
         for y in range(Y)

time: 77.5 us -> 77.5 us (level)
  no operation moved by 1% of the time
where the time goes in v19:
time: 77.5 us; the launch traced here: 77.3 us
  blocking collectives  74.3 us (96%)
  Pallas kernels  2.94 us (4%)
    all_to_all x2, blocking collectives, exchange(): lax.all_to_all(value, 'grp', 0, 0, tiled=True, axis_index_groups=PLANES)  53.9 us
    all_gather x1, blocking collectives, on_device(): lax.all_gather(partial, 'grp', axis_index_groups=couples(0))  13.2 us
    all_gather x1, blocking collectives, on_device(): pairs = lax.all_gather(pair, 'grp', axis_index_groups=couples(1))  7.15 us

profile of v19, /device:TPU:1, one launch (start us, length us, event | category | flops | bytes accessed | tf_op | source)
XLA Modules:
  0.0 77.3 jit_solution(1717669773331077581)
XLA Ops:
  0.0 1.3 %shard_map.37 = f32[1040,128]{1,0:T(8,128)S(1)} custom-call(s32[2,8]{1,0:T(2,128)} %table_hbm.1, s32[2]{0:T(128)} %coefs_hbm.1, f32[16,64,128]{2,1,0:T(8,128)} %bitcast.12), custom_call_target="tpu_custom_call" | custom-call | tf_op jit(solution)/shard_map/pallas_call | solution.py:162
  1.3 30.8 %all_to_all.10 = f32[16,1,8320]{2,1,0:T(1,128)S(1)} all-to-all(f32[16,1,8320]{2,1,0:T(1,128)S(1)} %bitcast.8), channel_id=1, replica_groups={{0,12,96,108,192,204,288,300,384,396,480,492,576,588,672,684},{24,36,12..., dimensions={0} | all-to-all | bytes 1064960 | tf_op jit(solution)/shard_map/all_to_all | solution.py:38
  32.1 0.3 shard_map.38
  32.4 13.2 %all-gather = f32[8,64,128]{2,1,0:T(8,128)S(1)} all-gather(f32[4,64,128]{2,1,0:T(8,128)S(1)} %get-tuple-element.7), channel_id=2, replica_groups={{0,24},{48,72},{36,60},{84,12},{96,120},{144,168},{132,156},{180,108},{..., dimensions={0}, use_global_device_ids=true | all-gather | bytes 393216 | tf_op jit(solution)/shard_map/all_gather | solution.py:187
  45.6 7.1 %all-gather.1 = f32[8,64,128]{2,1,0:T(8,128)S(1)} all-gather(f32[4,64,128]{2,1,0:T(8,128)S(1)} %reduce_sum.9), channel_id=3, replica_groups={{24,48},{72,0},{12,36},{60,84},{120,144},{168,96},{108,132},{156,180},{..., dimensions={0}, use_global_device_ids=true | all-gather | bytes 393216 | tf_op jit(solution)/shard_map/all_gather | solution.py:188
  52.8 0.4 shard_map.39
  53.2 23.1 %all_to_all.11 = f32[16,64,128]{2,1,0:T(8,128)S(1)} all-to-all(f32[16,64,128]{2,1,0:T(8,128)S(1)} %shard_map.39), channel_id=1, replica_groups={{0,12,96,108,192,204,288,300,384,396,480,492,576,588,672,684},{24,36,12..., dimensions={0} | all-to-all | bytes 1048576 | tf_op jit(solution)/shard_map/all_to_all | solution.py:38
  76.3 1.0 %shard_map.40 = f32[16,64,128]{2,1,0:T(8,128)} custom-call(f32[64,16,128]{2,1,0:T(8,128)S(1)} %bitcast.9), custom_call_target="tpu_custom_call" | custom-call | tf_op jit(solution)/shard_map/pallas_call | solution.py:197
  (1 shorter events, 0.0 us)

commit v20 on v16

--- a/solution.py
+++ b/solution.py
@@ -28,7 +28,7 @@
 ROWS = OWN * COUNT
 MESSAGE = ROWS + 1
 TILE = 8
-CHUNKS = 4
+CHUNKS = 2
 VMEM = pl.BlockSpec(memory_space=pltpu.VMEM)
 ROOM = pltpu.CompilerParams(vmem_limit_bytes=8 << 20)
 HBM = pl.BlockSpec(memory_space=pltpu.HBM)

time: 77.5 us -> 77.5 us (level)
  no operation moved by 1% of the time
where the time goes in v20:
time: 77.5 us; the launch traced here: 77.3 us
  blocking collectives  74.3 us (96%)
  Pallas kernels  2.99 us (4%)
    all_to_all x2, blocking collectives, exchange(): lax.all_to_all(value, 'grp', 0, 0, tiled=True, axis_index_groups=PLANES)  53.9 us
    all_gather x1, blocking collectives, on_device(): lax.all_gather(partial, 'grp', axis_index_groups=couples(0))  13.2 us
    all_gather x1, blocking collectives, on_device(): pairs = lax.all_gather(pair, 'grp', axis_index_groups=couples(1))  7.15 us

profile of v20, /device:TPU:1, one launch (start us, length us, event | category | flops | bytes accessed | tf_op | source)
XLA Modules:
  0.0 77.3 jit_solution(14619609012509613114)
XLA Ops:
  0.0 1.3 %shard_map.37 = f32[1040,128]{1,0:T(8,128)S(1)} custom-call(s32[2,8]{1,0:T(2,128)} %table_hbm.1, s32[2]{0:T(128)} %coefs_hbm.1, f32[16,64,128]{2,1,0:T(8,128)} %bitcast.12), custom_call_target="tpu_custom_call" | custom-call | tf_op jit(solution)/shard_map/pallas_call | solution.py:162
  1.3 30.8 %all_to_all.10 = f32[16,1,8320]{2,1,0:T(1,128)S(1)} all-to-all(f32[16,1,8320]{2,1,0:T(1,128)S(1)} %bitcast.8), channel_id=1, replica_groups={{0,12,96,108,192,204,288,300,384,396,480,492,576,588,672,684},{24,36,12..., dimensions={0} | all-to-all | bytes 1064960 | tf_op jit(solution)/shard_map/all_to_all | solution.py:38
  32.1 0.3 shard_map.38
  32.4 13.2 %all-gather = f32[8,64,128]{2,1,0:T(8,128)S(1)} all-gather(f32[4,64,128]{2,1,0:T(8,128)S(1)} %get-tuple-element.7), channel_id=2, replica_groups={{0,24},{48,72},{36,60},{12,84},{96,120},{144,168},{132,156},{108,180},{..., dimensions={0}, use_global_device_ids=true | all-gather | bytes 393216 | tf_op jit(solution)/shard_map/all_gather | solution.py:187
  45.7 7.2 %all-gather.1 = f32[8,64,128]{2,1,0:T(8,128)S(1)} all-gather(f32[4,64,128]{2,1,0:T(8,128)S(1)} %reduce_sum.9), channel_id=3, replica_groups={{24,48},{0,72},{12,36},{60,84},{120,144},{96,168},{108,132},{156,180},{..., dimensions={0}, use_global_device_ids=true | all-gather | bytes 393216 | tf_op jit(solution)/shard_map/all_gather | solution.py:188
  52.8 0.4 shard_map.39
  53.2 23.1 %all_to_all.11 = f32[16,64,128]{2,1,0:T(8,128)S(1)} all-to-all(f32[16,64,128]{2,1,0:T(8,128)S(1)} %shard_map.39), channel_id=1, replica_groups={{0,12,96,108,192,204,288,300,384,396,480,492,576,588,672,684},{24,36,12..., dimensions={0} | all-to-all | bytes 1048576 | tf_op jit(solution)/shard_map/all_to_all | solution.py:38
  76.3 1.0 %shard_map.40 = f32[16,64,128]{2,1,0:T(8,128)} custom-call(f32[64,16,128]{2,1,0:T(8,128)S(1)} %bitcast.9), custom_call_target="tpu_custom_call" | custom-call | tf_op jit(solution)/shard_map/pallas_call | solution.py:197
  (1 shorter events, 0.0 us)
